TPU v7x, 256 devices: a whole 4x4x8 slice. The times are simulated.
256 devices in a mesh: dp: 8 (over z), ctx: 16 (over x, y_hi, core), kvh: 2 (over y_lo).
Axes of the slice: x: 4, y: 4 (y_hi: 2, y_lo: 2; y = y_hi * 2 + y_lo), z: 8, core: 2. Of those that a mesh axis runs over, the one named last changes fastest.
Arguments:
- query_heads: bfloat16 [16384, 1792], P(('dp', 'ctx', 'kvh')), may hold values from -210 to 210
- key_heads: bfloat16 [16384, 256], P(('dp', 'ctx', 'kvh')), may hold values from -7 to 7
- pool_values: bfloat16 [16384, 256], P(('dp', 'ctx', 'kvh')), may hold values from -6 to 6
- output_grad: bfloat16 [16384, 1792], P(('dp', 'ctx', 'kvh')), may hold values from -6 to 6
- lengths: int32 [8, 4], replicated, may hold values from 1 to 1024, 2048 in all within a row
- placement: int32 [16384], P(('dp', 'ctx')), may hold values from 0 to 15, as said below
Outputs:
- attended: bfloat16 [32768, 1792], P(('dp', 'ctx'), 'kvh')
- grad_query: bfloat16 [32768, 1792], P(('dp', 'ctx'), 'kvh')
- key_gradient: bfloat16 [32768, 256], P(('dp', 'ctx'), 'kvh')
- value_gradient: bfloat16 [32768, 256], P(('dp', 'ctx'), 'kvh')
Inputs may be any that keep to these rules, and one draw needn't show every extreme that they name: `placement`: of the 128 rows of one pool block, at most 16 have one destination; in every group one destination receives exactly 16 rows from every block of the group, so that one trainer device of each group receives 256 rows.
All inputs are finite; a program needn't handle non-finite values.
Results may differ from a plain program's by a relative error of at most 0.034.
Values may be sent and summed in bfloat16 or wider, within the bound.
No kernel may reach another device: no remote copies, remote signals or barrier semaphores. Data moves between devices by JAX's collectives and lax.ppermute only.
A program may use at most 128 MiB of HBM per device.

v0:
```python
import math

import jax
import jax.numpy as jnp
from jax import lax
from jax.sharding import PartitionSpec as P

HEAD_DIMENSION = 128


MASKED_LOGIT = -1e30


def for_sending(array):
    return jax.tree.map(lambda a: a.astype(jnp.bfloat16) if a.dtype == jnp.float32 else a, array)


def from_behind(value, axis, steps):
    count = lax.axis_size(axis)
    pairs = [(source, (source + steps) % count) for source in range(count)]
    return lax.ppermute(value, axis, pairs)


def rollout_marks(lengths, trainer_group, ctx_pos, tok_rows):
    position = ctx_pos * tok_rows + jnp.arange(tok_rows, dtype=jnp.int32)
    rollout_len = lengths[trainer_group]
    rollout_end = jnp.cumsum(rollout_len)
    begins = rollout_end - rollout_len
    inside = (position[:, None] >= begins[None, :]) & (position[:, None] < rollout_end[None, :])
    starts = jnp.sum(jnp.where(inside, begins[None, :], 0), axis=1)
    return (starts, position)


def visible_pairs(starts_query, position_query, starts_key, position_key):
    same_rollout = starts_query[:, None] == starts_key[None, :]
    causal = position_key[None, :] <= position_query[:, None]
    return same_rollout & causal & (starts_key[None, :] >= 0)


def shards(query_heads, key_heads, pool_values, output_grad, lengths, placement):
    dp_count = lax.axis_size("dp")
    ctx_count = lax.axis_size("ctx")
    dp_pos = lax.axis_index("dp")
    ctx_pos = lax.axis_index("ctx")
    query_rows, key_rows, value_rows, grad_rows = (
        lax.all_to_all(query_heads, "kvh", split_axis=1, concat_axis=0, tiled=True),
        lax.all_to_all(key_heads, "kvh", split_axis=1, concat_axis=0, tiled=True),
        lax.all_to_all(pool_values, "kvh", split_axis=1, concat_axis=0, tiled=True),
        lax.all_to_all(output_grad, "kvh", split_axis=1, concat_axis=0, tiled=True),
    )
    tok_rows = placement.shape[0]
    capacity = 2 * tok_rows // ctx_count
    slot_count = ctx_count * capacity
    trainer_group = (dp_pos + ctx_pos) % dp_count
    starts, position = rollout_marks(lengths, trainer_group, ctx_pos, tok_rows)
    destinations = jnp.arange(ctx_count, dtype=jnp.int32)
    onehot = (placement[:, None] == destinations[None, :]).astype(jnp.int32)
    earlier = jnp.sum((jnp.cumsum(onehot, axis=0) - onehot) * onehot, axis=1)
    slot_of_row = placement * capacity + earlier
    source_row = (
        jnp.full((slot_count,), tok_rows, jnp.int32)
        .at[slot_of_row]
        .set(jnp.arange(tok_rows, dtype=jnp.int32))
    )

    def bucket(table_rows, filler):
        padded = jnp.concatenate(
            [table_rows, jnp.full((1,) + table_rows.shape[1:], filler, table_rows.dtype)], axis=0
        )
        return jnp.take(padded, source_row, axis=0).reshape(
            (ctx_count, capacity) + table_rows.shape[1:]
        )

    outgoing = (
        bucket(query_rows, 0),
        bucket(key_rows, 0),
        bucket(value_rows, 0),
        bucket(grad_rows, 0),
        bucket(starts, -1),
        bucket(position, -1),
    )
    sources = jnp.arange(ctx_count, dtype=jnp.int32)
    owners_mask = jnp.arange(dp_count, dtype=jnp.int32) == trainer_group

    def spread(member):
        marker = owners_mask.reshape((dp_count,) + (1,) * member.ndim)
        widened = jnp.where(marker, member[None], jnp.zeros_like(member)[None])
        return widened.reshape((dp_count * ctx_count,) + member.shape[1:])

    landed = (
        lax.all_to_all(spread(outgoing[0]), ("dp", "ctx"), split_axis=0, concat_axis=0, tiled=True),
        lax.all_to_all(spread(outgoing[1]), ("dp", "ctx"), split_axis=0, concat_axis=0, tiled=True),
        lax.all_to_all(spread(outgoing[2]), ("dp", "ctx"), split_axis=0, concat_axis=0, tiled=True),
        lax.all_to_all(spread(outgoing[3]), ("dp", "ctx"), split_axis=0, concat_axis=0, tiled=True),
        lax.all_to_all(spread(outgoing[4]), ("dp", "ctx"), split_axis=0, concat_axis=0, tiled=True),
        lax.all_to_all(spread(outgoing[5]), ("dp", "ctx"), split_axis=0, concat_axis=0, tiled=True),
    )
    chosen = (dp_pos - sources) % dp_count * ctx_count + sources
    arrived = [jnp.take(member, chosen, axis=0) for member in landed]
    query_slots = arrived[0].reshape(slot_count, -1)
    key_slots = arrived[1].reshape(slot_count, -1)
    value_slots = arrived[2].reshape(slot_count, -1)
    grad_slots = arrived[3].reshape(slot_count, -1)
    start_slots = arrived[4].reshape(slot_count)
    position_slots = arrived[5].reshape(slot_count)
    head_size = HEAD_DIMENSION
    kv_heads = key_slots.shape[1] // head_size
    queries_per_group = query_slots.shape[1] // key_slots.shape[1]
    scaling = 1.0 / math.sqrt(head_size)
    query_split = query_slots.reshape(slot_count, kv_heads, queries_per_group, head_size)
    grad_split = grad_slots.reshape(slot_count, kv_heads, queries_per_group, head_size)
    filled = start_slots >= 0

    def logits_for(key_piece, start_piece, position_piece):
        key_split = key_piece.reshape(key_piece.shape[0], kv_heads, head_size)
        logits = (
            jnp.einsum("qjgd,kjd->jgqk", query_split, key_split, preferred_element_type=jnp.float32)
            * scaling
        )
        visible = visible_pairs(start_slots, position_slots, start_piece, position_piece)[
            None, None
        ]
        return (logits, visible, key_split)

    row_top = jnp.full((kv_heads, queries_per_group, slot_count), MASKED_LOGIT, jnp.float32)
    key_piece = lax.all_gather(key_slots, "ctx", axis=0, tiled=True)
    value_piece = lax.all_gather(value_slots, "ctx", axis=0, tiled=True)
    start_piece = lax.all_gather(for_sending(start_slots), "ctx", axis=0, tiled=True)
    position_piece = lax.all_gather(for_sending(position_slots), "ctx", axis=0, tiled=True)
    logits, visible, key_split = logits_for(key_piece, start_piece, position_piece)
    value_split = value_piece.reshape(value_piece.shape[0], kv_heads, head_size)
    new_top = jnp.maximum(row_top, jnp.max(jnp.where(visible, logits, MASKED_LOGIT), axis=-1))
    expo = jnp.where(visible, jnp.exp(logits - new_top[..., None]), 0.0)
    row_total = jnp.sum(expo, axis=-1)
    weighted = jnp.einsum(
        "jgqk,kjd->jgqd", expo.astype(jnp.bfloat16), value_split, preferred_element_type=jnp.float32
    )
    running = (new_top, row_total, weighted)
    row_top, row_total, weighted = running
    safe_total = jnp.where(filled[None, None], row_total, 1.0)
    attended = (
        (weighted / safe_total[..., None])
        .transpose(2, 0, 1, 3)
        .reshape(slot_count, -1)
        .astype(jnp.bfloat16)
    )
    lse = row_top + jnp.log(safe_total)
    attended_wide = lax.optimization_barrier(attended).astype(jnp.float32)
    delta = jnp.sum(
        (grad_slots.astype(jnp.float32) * attended_wide).reshape(
            slot_count, kv_heads, queries_per_group, head_size
        ),
        axis=-1,
    ).transpose(1, 2, 0)

    def backward_piece(key_piece, value_piece, start_piece, position_piece):
        row_count = key_piece.shape[0]
        logits, visible, key_split = logits_for(key_piece, start_piece, position_piece)
        value_split = value_piece.reshape(row_count, kv_heads, head_size)
        weights = jnp.where(visible, jnp.exp(logits - lse[..., None]), 0.0)
        value_term = jnp.einsum(
            "jgqk,qjgd->kjd",
            weights.astype(jnp.bfloat16),
            grad_split,
            preferred_element_type=jnp.float32,
        ).reshape(row_count, -1)
        dprob = jnp.einsum(
            "qjgd,kjd->jgqk", grad_split, value_split, preferred_element_type=jnp.float32
        )
        dlogits = (weights * (dprob - delta[..., None])).astype(jnp.bfloat16)
        query_term = (
            jnp.einsum("jgqk,kjd->qjgd", dlogits, key_split, preferred_element_type=jnp.float32)
            * scaling
        )
        key_term = (
            jnp.einsum("jgqk,qjgd->kjd", dlogits, query_split, preferred_element_type=jnp.float32)
            * scaling
        ).reshape(row_count, -1)
        return (query_term, key_term, value_term)

    query_zero = jnp.zeros(query_split.shape, jnp.float32)

    def cycle_step(step_id, cycle_state):
        query_sum, key_now, value_now, start_now, position_now, key_sum, value_sum = cycle_state
        query_term, key_term, value_term = backward_piece(
            key_now, value_now, start_now, position_now
        )
        moved = (
            from_behind(key_now, "ctx", 1),
            from_behind(value_now, "ctx", 1),
            from_behind(for_sending(start_now), "ctx", 1).astype(start_now.dtype),
            from_behind(for_sending(position_now), "ctx", 1).astype(position_now.dtype),
            from_behind((key_sum + key_term).astype(jnp.bfloat16), "ctx", 1).astype(jnp.float32),
            from_behind((value_sum + value_term).astype(jnp.bfloat16), "ctx", 1).astype(
                jnp.float32
            ),
        )
        return (query_sum + query_term,) + tuple(moved)

    kv_zero = jnp.zeros(key_slots.shape, jnp.float32)
    cycle_state = lax.fori_loop(
        0,
        ctx_count,
        cycle_step,
        (query_zero, key_slots, value_slots, start_slots, position_slots, kv_zero, kv_zero),
    )
    query_sum = cycle_state[0]
    key_sum = cycle_state[5]
    value_sum = cycle_state[6]
    grad_query = query_sum.reshape(slot_count, -1).astype(jnp.bfloat16)
    return (attended, grad_query, key_sum.astype(jnp.bfloat16), value_sum.astype(jnp.bfloat16))


def solution(mesh):
    in_specs = (
        P(("dp", "ctx", "kvh"), None),
        P(("dp", "ctx", "kvh"), None),
        P(("dp", "ctx", "kvh"), None),
        P(("dp", "ctx", "kvh"), None),
        P(),
        P(("dp", "ctx")),
    )
    out_specs = (
        P(("dp", "ctx"), "kvh"),
        P(("dp", "ctx"), "kvh"),
        P(("dp", "ctx"), "kvh"),
        P(("dp", "ctx"), "kvh"),
    )
    return jax.shard_map(shards, mesh=mesh, in_specs=in_specs, out_specs=out_specs, check_vma=False)
```

profile of v0, /device:TPU:1, one launch (start us, length us, event | category | flops | bytes accessed | tf_op | source)
XLA Modules:
  0.0 697.2 jit_solution(6001636338062987005)
XLA Ops:
  17.0 27.9 %all_to_all.114 = s32[128,1,16]{2,1,0:T(1,128)S(1)} all-to-all(s32[128,1,16]{2,1,0:T(1,128)S(1)} %get-tuple-element.267), channel_id=1, replica_groups=mesh['dp'=8,'ctx'=16,'kvh'=2] {'dp','ctx'}, dimensions={0} | all-to-all | bytes 16384 | tf_op jit(solution)/shard_map/all_to_all | solution.py:96
  44.9 6.2 all-to-all-start
  51.8 11.2 %all-to-all-done = s32[128,1,16]{2,1,0:T(1,128)S(1)} async-done(((s32[128,1,16]{2,1,0:T(1,128)}), s32[128,1,16]{2,1,0:T(1,128)S(1)}, u32[]{:S(2)}, u32[]{:S(2)}) %all-to-all-start) | async-done | bytes 8224 | tf_op jit(solution)/shard_map/all_to_all | solution.py:95
  89.6 30.5 %all_to_all.115 = bf16[128,16,128]{2,1,0:T(8,128)(2,1)S(1)} all-to-all(bf16[128,16,128]{2,1,0:T(8,128)(2,1)S(1)} %get-tuple-element.261), channel_id=1, replica_groups=mesh['dp'=8,'ctx'=16,'kvh'=2] {'dp','ctx'}, dimensions={0} | all-to-all | bytes 1048576 | tf_op jit(solution)/shard_map/all_to_all | solution.py:92
  120.1 7.3 %all-to-all-start.7 = ((bf16[128,16,128]{2,1,0:T(8,128)(2,1)}), bf16[128,16,128]{2,1,0:T(8,128)(2,1)S(1)}, u32[]{:S(2)}, u32[]{:S(2)}) async-start(bf16[128,16,128]{2,1,0:T(8,128)(2,1)} %get-tuple-element.260), calls=%async_computation.7 | async-start | bytes 1048576 | tf_op jit(solution)/shard_map/all_to_all | solution.py:93
  133.5 14.2 %all-to-all-done.7 = bf16[128,16,128]{2,1,0:T(8,128)(2,1)S(1)} async-done(((bf16[128,16,128]{2,1,0:T(8,128)(2,1)}), bf16[128,16,128]{2,1,0:T(8,128)(2,1)S(1)}, u32[]{:S(2)}, u32[]{:S(2)}) %all-to-all-start.7) | async-done | bytes 524320 | tf_op jit(solution)/shard_map/all_to_all | solution.py:93
  147.7 92.6 %all_to_all.116 = bf16[128,16,896]{2,1,0:T(8,128)(2,1)} all-to-all(bf16[128,16,896]{2,1,0:T(8,128)(2,1)} %get-tuple-element.255), channel_id=1, replica_groups=mesh['dp'=8,'ctx'=16,'kvh'=2] {'dp','ctx'}, dimensions={0} | all-to-all | bytes 7340032 | tf_op jit(solution)/shard_map/all_to_all | solution.py:91
  240.3 9.9 %all-to-all-start.9 = ((bf16[128,16,896]{2,1,0:T(8,128)(2,1)}), bf16[128,16,896]{2,1,0:T(8,128)(2,1)}, u32[]{:S(2)}, u32[]{:S(2)}) async-start(bf16[128,16,896]{2,1,0:T(8,128)(2,1)} %get-tuple-element.254), calls=%async_computation.9 | async-start | bytes 7340032 | tf_op jit(solution)/shard_map/all_to_all | solution.py:94
  254.0 24.5 %all-gather = s32[16,1,256]{2,1,0:T(1,128)S(1)} all-gather(s32[1,1,256]{2,1,0:T(1,128)S(1)} %reshape.646), channel_id=1, replica_groups=mesh['dp'=8,'ctx'=16,'kvh'=2] {'ctx'}, dimensions={0}, use_global_device_ids=true | all-gather | bytes 17408 | tf_op jit(solution)/shard_map/all_gather | solution.py:128
  278.4 20.0 %all-gather.1 = s32[16,1,256]{2,1,0:T(1,128)S(1)} all-gather(s32[1,1,256]{2,1,0:T(1,128)S(1)} %reshape.648), channel_id=1, replica_groups=mesh['dp'=8,'ctx'=16,'kvh'=2] {'ctx'}, dimensions={0}, use_global_device_ids=true | all-gather | bytes 17408 | tf_op jit(solution)/shard_map/all_gather | solution.py:129
  306.1 28.0 %all-to-all-done.9 = bf16[128,16,896]{2,1,0:T(8,128)(2,1)} async-done(((bf16[128,16,896]{2,1,0:T(8,128)(2,1)}), bf16[128,16,896]{2,1,0:T(8,128)(2,1)}, u32[]{:S(2)}, u32[]{:S(2)}) %all-to-all-start.9) | async-done | bytes 3670048 | tf_op jit(solution)/shard_map/all_to_all | solution.py:94
  341.5 13.2 %fusion.21 = (f32[7,256]{1,0:T(8,128)S(1)}, f32[4096,256,7]{1,0,2:T(8,128)}) fusion(pred[256,4096]{0,1:T(8,128)(4,1)S(1)} %and_and_fusion.1, bf16[256,7,128]{2,1,0:T(8,128)(2,1)} %reshape.524, bf16[4096,128]{1,0:T(8,128)(2,1)} %all-gather.5.cloned.1.call-done), kind=kOutput, calls=%fused_computation.43 | convolution fusion | flops 1901066496 | bytes 31923200 | tf_op jit(solution)/shard_map/qjgd,kjd->jgqk/dot_general | solution.py:117
  354.7 12.9 %fusion.24 = f32[7,256]{1,0:T(8,128)S(1)} fusion(f32[4096,256,7]{1,0,2:T(8,128)} %get-tuple-element.269, f32[7,256]{1,0:T(8,128)S(1)} %broadcast_maximum_fusion, pred[256,4096]{0,1:T(8,128)(4,1)S(1)} %and_and_fusion.1), kind=kLoop, calls=%fused_computation.46 | loop fusion | flops 29358336 | bytes 30423040 | tf_op jit(solution)/shard_map/reduce_sum | solution.py:134
  367.7 12.7 %fusion.38 = bf16[7,256,128]{1,2,0:T(8,128)(2,1)S(1)} fusion(f32[4096,256,7]{1,0,2:T(8,128)} %get-tuple-element.269, f32[7,256]{1,0:T(8,128)S(1)} %broadcast_maximum_fusion, pred[256,4096]{0,1:T(8,128)(4,1)S(1)} %and_and_fusion.1, bf16[4096,128]{0,1:T(8,128)(2,1)} %all-gather.7.cloned.1.call-done, f32[7,256]{1,0:T(8,128)S(1)} %broadcast_select_fusion.12), kind=kOutput, calls=%fused_computation.58 | convolution fusion | flops 1908867072 | bytes 31930368 | tf_op jit(solution)/shard_map/jgqk,kjd->jgqd/dot_general | solution.py:135
  389.3 298.6 %while.24 = (s32[]{:T(128)}, f32[256,1,7,128]{3,0,2,1:T(8,128)S(1)}, bf16[256,128]{1,0:T(8,128)(2,1)S(1)}, bf16[256,128]{1,0:T(8,128)(2,1)S(1)}, s32[256]{0:T(25...) while((s32[]{:T(128)}, ...), condition=%wide.wide.region_9.16_spmd.clone, body=%wide.wide.region_8.15_spmd.clone.sunk | while | flops 591659264 | bytes 14385057 | solution.py:201
  445.4 4.8 collective-permute-start.1
  465.8 4.8 collective-permute-start.1
  486.0 4.8 collective-permute-start.1
  521.3 4.8 collective-permute-start.1
  541.6 4.8 collective-permute-start.1
  561.8 4.8 collective-permute-start.1
  597.1 4.8 collective-permute-start.1
  617.4 4.8 collective-permute-start.1
  637.6 4.8 collective-permute-start.1
  (504 shorter events, 326.9 us)
Async XLA Ops:
  44.9 18.0 %all-to-all-start = ((s32[128,1,16]{2,1,0:T(1,128)}), s32[128,1,16]{2,1,0:T(1,128)S(1)}, u32[]{:S(2)}, u32[]{:S(2)}) async-start(s32[128,1,16]{2,1,0:T(1,128)} %get-tuple-element.266), calls=%async_computation | async-start | bytes 131072 | tf_op jit(solution)/shard_map/all_to_all | solution.py:95
  120.1 27.6 %all-to-all-start.7 = ((bf16[128,16,128]{2,1,0:T(8,128)(2,1)}), bf16[128,16,128]{2,1,0:T(8,128)(2,1)S(1)}, u32[]{:S(2)}, u32[]{:S(2)}) async-start(bf16[128,16,128]{2,1,0:T(8,128)(2,1)} %get-tuple-element.260), calls=%async_computation.7 | async-start | bytes 1048576 | tf_op jit(solution)/shard_map/all_to_all | solution.py:93
  240.3 93.8 %all-to-all-start.9 = ((bf16[128,16,896]{2,1,0:T(8,128)(2,1)}), bf16[128,16,896]{2,1,0:T(8,128)(2,1)}, u32[]{:S(2)}, u32[]{:S(2)}) async-start(bf16[128,16,896]{2,1,0:T(8,128)(2,1)} %get-tuple-element.254), calls=%async_computation.9 | async-start | bytes 7340032 | tf_op jit(solution)/shard_map/all_to_all | solution.py:94
  250.2 91.3 %all-gather.5.cloned.1.call-start = ((), (), s32[]{:S(2)}) async-start(), calls=%async_computation.10 | async-start | bytes 1114112 | tf_op jit(solution)/shard_map/all_gather | solution.py:126
  252.2 115.5 %all-gather.7.cloned.1.call-start = ((), (), s32[]{:S(2)}) async-start(), calls=%async_computation.11 | async-start | bytes 1114112 | tf_op jit(solution)/shard_map/all_gather | solution.py:127
  406.2 19.0 %collective-permute-start = (bf16[256,128]{1,0:T(8,128)(2,1)S(1)}, bf16[256,128]{1,0:T(8,128)(2,1)S(1)}, u32[]{:S(2)}, u32[]{:S(2)}) collective-permute-start(bf16[256,128]{1,0:T(8,128)(2,1)S(1)} %copy.110), channel_id=1, source_target_pairs={{0,2},{2,4},{4,6},{6,8},{8,10},{10,12},{12,14},{14,16},{16,18},{18... | collective-permute-start | bytes 196616 | tf_op jit(solution)/shard_map/while/body/eval_jaxpr/ppermute | solution.py:21
  425.2 17.1 %collective-permute-start = (bf16[256,128]{1,0:T(8,128)(2,1)S(1)}, bf16[256,128]{1,0:T(8,128)(2,1)S(1)}, u32[]{:S(2)}, u32[]{:S(2)}) collective-permute-start(bf16[256,128]{1,0:T(8,128)(2,1)S(1)} %copy.110), channel_id=1, source_target_pairs={{0,2},{2,4},{4,6},{6,8},{8,10},{10,12},{12,14},{14,16},{16,18},{18... | collective-permute-start | bytes 196616 | tf_op jit(solution)/shard_map/while/body/eval_jaxpr/ppermute | solution.py:21
  442.4 18.1 %collective-permute-start = (bf16[256,128]{1,0:T(8,128)(2,1)S(1)}, bf16[256,128]{1,0:T(8,128)(2,1)S(1)}, u32[]{:S(2)}, u32[]{:S(2)}) collective-permute-start(bf16[256,128]{1,0:T(8,128)(2,1)S(1)} %copy.110), channel_id=1, source_target_pairs={{0,2},{2,4},{4,6},{6,8},{8,10},{10,12},{12,14},{14,16},{16,18},{18... | collective-permute-start | bytes 196616 | tf_op jit(solution)/shard_map/while/body/eval_jaxpr/ppermute | solution.py:21
  460.5 20.3 %collective-permute-start = (bf16[256,128]{1,0:T(8,128)(2,1)S(1)}, bf16[256,128]{1,0:T(8,128)(2,1)S(1)}, u32[]{:S(2)}, u32[]{:S(2)}) collective-permute-start(bf16[256,128]{1,0:T(8,128)(2,1)S(1)} %copy.110), channel_id=1, source_target_pairs={{0,2},{2,4},{4,6},{6,8},{8,10},{10,12},{12,14},{14,16},{16,18},{18... | collective-permute-start | bytes 196616 | tf_op jit(solution)/shard_map/while/body/eval_jaxpr/ppermute | solution.py:21
  462.6 18.1 %collective-permute-start.2 = (s32[256]{0:T(256)S(1)}, s32[256]{0:T(256)S(1)}, u32[]{:S(2)}, u32[]{:S(2)}) collective-permute-start(s32[256]{0:T(256)S(1)} %copy.112), channel_id=1, source_target_pairs={{0,2},{2,4},{4,6},{6,8},{8,10},{10,12},{12,14},{14,16},{16,18},{18... | collective-permute-start | bytes 3080 | tf_op jit(solution)/shard_map/while/body/eval_jaxpr/ppermute | solution.py:21
  480.8 20.2 %collective-permute-start = (bf16[256,128]{1,0:T(8,128)(2,1)S(1)}, bf16[256,128]{1,0:T(8,128)(2,1)S(1)}, u32[]{:S(2)}, u32[]{:S(2)}) collective-permute-start(bf16[256,128]{1,0:T(8,128)(2,1)S(1)} %copy.110), channel_id=1, source_target_pairs={{0,2},{2,4},{4,6},{6,8},{8,10},{10,12},{12,14},{14,16},{16,18},{18... | collective-permute-start | bytes 196616 | tf_op jit(solution)/shard_map/while/body/eval_jaxpr/ppermute | solution.py:21
  482.9 18.0 %collective-permute-start.2 = (s32[256]{0:T(256)S(1)}, s32[256]{0:T(256)S(1)}, u32[]{:S(2)}, u32[]{:S(2)}) collective-permute-start(s32[256]{0:T(256)S(1)} %copy.112), channel_id=1, source_target_pairs={{0,2},{2,4},{4,6},{6,8},{8,10},{10,12},{12,14},{14,16},{16,18},{18... | collective-permute-start | bytes 3080 | tf_op jit(solution)/shard_map/while/body/eval_jaxpr/ppermute | solution.py:21
  501.0 17.1 %collective-permute-start = (bf16[256,128]{1,0:T(8,128)(2,1)S(1)}, bf16[256,128]{1,0:T(8,128)(2,1)S(1)}, u32[]{:S(2)}, u32[]{:S(2)}) collective-permute-start(bf16[256,128]{1,0:T(8,128)(2,1)S(1)} %copy.110), channel_id=1, source_target_pairs={{0,2},{2,4},{4,6},{6,8},{8,10},{10,12},{12,14},{14,16},{16,18},{18... | collective-permute-start | bytes 196616 | tf_op jit(solution)/shard_map/while/body/eval_jaxpr/ppermute | solution.py:21
  518.2 18.1 %collective-permute-start = (bf16[256,128]{1,0:T(8,128)(2,1)S(1)}, bf16[256,128]{1,0:T(8,128)(2,1)S(1)}, u32[]{:S(2)}, u32[]{:S(2)}) collective-permute-start(bf16[256,128]{1,0:T(8,128)(2,1)S(1)} %copy.110), channel_id=1, source_target_pairs={{0,2},{2,4},{4,6},{6,8},{8,10},{10,12},{12,14},{14,16},{16,18},{18... | collective-permute-start | bytes 196616 | tf_op jit(solution)/shard_map/while/body/eval_jaxpr/ppermute | solution.py:21
  536.3 20.3 %collective-permute-start = (bf16[256,128]{1,0:T(8,128)(2,1)S(1)}, bf16[256,128]{1,0:T(8,128)(2,1)S(1)}, u32[]{:S(2)}, u32[]{:S(2)}) collective-permute-start(bf16[256,128]{1,0:T(8,128)(2,1)S(1)} %copy.110), channel_id=1, source_target_pairs={{0,2},{2,4},{4,6},{6,8},{8,10},{10,12},{12,14},{14,16},{16,18},{18... | collective-permute-start | bytes 196616 | tf_op jit(solution)/shard_map/while/body/eval_jaxpr/ppermute | solution.py:21
  538.4 18.1 %collective-permute-start.2 = (s32[256]{0:T(256)S(1)}, s32[256]{0:T(256)S(1)}, u32[]{:S(2)}, u32[]{:S(2)}) collective-permute-start(s32[256]{0:T(256)S(1)} %copy.112), channel_id=1, source_target_pairs={{0,2},{2,4},{4,6},{6,8},{8,10},{10,12},{12,14},{14,16},{16,18},{18... | collective-permute-start | bytes 3080 | tf_op jit(solution)/shard_map/while/body/eval_jaxpr/ppermute | solution.py:21
  556.6 20.2 %collective-permute-start = (bf16[256,128]{1,0:T(8,128)(2,1)S(1)}, bf16[256,128]{1,0:T(8,128)(2,1)S(1)}, u32[]{:S(2)}, u32[]{:S(2)}) collective-permute-start(bf16[256,128]{1,0:T(8,128)(2,1)S(1)} %copy.110), channel_id=1, source_target_pairs={{0,2},{2,4},{4,6},{6,8},{8,10},{10,12},{12,14},{14,16},{16,18},{18... | collective-permute-start | bytes 196616 | tf_op jit(solution)/shard_map/while/body/eval_jaxpr/ppermute | solution.py:21
  558.8 18.0 %collective-permute-start.2 = (s32[256]{0:T(256)S(1)}, s32[256]{0:T(256)S(1)}, u32[]{:S(2)}, u32[]{:S(2)}) collective-permute-start(s32[256]{0:T(256)S(1)} %copy.112), channel_id=1, source_target_pairs={{0,2},{2,4},{4,6},{6,8},{8,10},{10,12},{12,14},{14,16},{16,18},{18... | collective-permute-start | bytes 3080 | tf_op jit(solution)/shard_map/while/body/eval_jaxpr/ppermute | solution.py:21
  594.0 18.1 %collective-permute-start = (bf16[256,128]{1,0:T(8,128)(2,1)S(1)}, bf16[256,128]{1,0:T(8,128)(2,1)S(1)}, u32[]{:S(2)}, u32[]{:S(2)}) collective-permute-start(bf16[256,128]{1,0:T(8,128)(2,1)S(1)} %copy.110), channel_id=1, source_target_pairs={{0,2},{2,4},{4,6},{6,8},{8,10},{10,12},{12,14},{14,16},{16,18},{18... | collective-permute-start | bytes 196616 | tf_op jit(solution)/shard_map/while/body/eval_jaxpr/ppermute | solution.py:21
  612.1 20.3 %collective-permute-start = (bf16[256,128]{1,0:T(8,128)(2,1)S(1)}, bf16[256,128]{1,0:T(8,128)(2,1)S(1)}, u32[]{:S(2)}, u32[]{:S(2)}) collective-permute-start(bf16[256,128]{1,0:T(8,128)(2,1)S(1)} %copy.110), channel_id=1, source_target_pairs={{0,2},{2,4},{4,6},{6,8},{8,10},{10,12},{12,14},{14,16},{16,18},{18... | collective-permute-start | bytes 196616 | tf_op jit(solution)/shard_map/while/body/eval_jaxpr/ppermute | solution.py:21
  614.2 18.1 %collective-permute-start.2 = (s32[256]{0:T(256)S(1)}, s32[256]{0:T(256)S(1)}, u32[]{:S(2)}, u32[]{:S(2)}) collective-permute-start(s32[256]{0:T(256)S(1)} %copy.112), channel_id=1, source_target_pairs={{0,2},{2,4},{4,6},{6,8},{8,10},{10,12},{12,14},{14,16},{16,18},{18... | collective-permute-start | bytes 3080 | tf_op jit(solution)/shard_map/while/body/eval_jaxpr/ppermute | solution.py:21
  632.5 20.2 %collective-permute-start = (bf16[256,128]{1,0:T(8,128)(2,1)S(1)}, bf16[256,128]{1,0:T(8,128)(2,1)S(1)}, u32[]{:S(2)}, u32[]{:S(2)}) collective-permute-start(bf16[256,128]{1,0:T(8,128)(2,1)S(1)} %copy.110), channel_id=1, source_target_pairs={{0,2},{2,4},{4,6},{6,8},{8,10},{10,12},{12,14},{14,16},{16,18},{18... | collective-permute-start | bytes 196616 | tf_op jit(solution)/shard_map/while/body/eval_jaxpr/ppermute | solution.py:21
  634.6 18.0 %collective-permute-start.2 = (s32[256]{0:T(256)S(1)}, s32[256]{0:T(256)S(1)}, u32[]{:S(2)}, u32[]{:S(2)}) collective-permute-start(s32[256]{0:T(256)S(1)} %copy.112), channel_id=1, source_target_pairs={{0,2},{2,4},{4,6},{6,8},{8,10},{10,12},{12,14},{14,16},{16,18},{18... | collective-permute-start | bytes 3080 | tf_op jit(solution)/shard_map/while/body/eval_jaxpr/ppermute | solution.py:21
  669.8 18.1 %collective-permute-start = (bf16[256,128]{1,0:T(8,128)(2,1)S(1)}, bf16[256,128]{1,0:T(8,128)(2,1)S(1)}, u32[]{:S(2)}, u32[]{:S(2)}) collective-permute-start(bf16[256,128]{1,0:T(8,128)(2,1)S(1)} %copy.110), channel_id=1, source_target_pairs={{0,2},{2,4},{4,6},{6,8},{8,10},{10,12},{12,14},{14,16},{16,18},{18... | collective-permute-start | bytes 196616 | tf_op jit(solution)/shard_map/while/body/eval_jaxpr/ppermute | solution.py:21
  (88 other events, 1096.8 us)
Sparse Core Ops, SparseCore 0:
  254.3 55.3 all-gather.4
  312.9 51.3 all-gather.6
where the time goes:
time: 704 us; the launch traced here: 697 us
  starting transfers between devices  239 us (34%)
  blocking collectives  195 us (28%)
  waiting for transfers between devices  111 us (16%)
  matrix products  65.8 us (9%)
  local copies, waits for them, and re-layouts  36.7 us (5%)
  other arithmetic  32.6 us (5%)
  between operations  14.5 us (2%)
    ppermute x96, starting transfers between devices, from_behind(): return lax.ppermute(value, axis, pairs)  202 us
    all_to_all x1, blocking collectives, shards(): lax.all_to_all(spread(outgoing[0]), ('dp', 'ctx'), split_axis=0, concat_a...  92.6 us
    ppermute x96, waiting for transfers between devices, from_behind(): return lax.ppermute(value, axis, pairs)  51.3 us
    all_to_all x1, blocking collectives, shards(): lax.all_to_all(spread(outgoing[1]), ('dp', 'ctx'), split_axis=0, concat_a...  30.5 us
    all_to_all x1, waiting for transfers between devices, shards(): lax.all_to_all(spread(outgoing[3]), ('dp', 'ctx'), split_axis=0, concat_a...  28 us
    all_to_all x1, blocking collectives, shards(): lax.all_to_all(spread(outgoing[5]), ('dp', 'ctx'), split_axis=0, concat_a...  27.9 us
    all_gather x1, blocking collectives, shards(): lax.all_gather(for_sending(start_slots), 'ctx', axis=0, tiled=True)  24.5 us
    dot_general x17, matrix products, logits_for(): jnp.einsum('qjgd,kjd->jgqk', query_split, key_split, preferred_element_ty...  22 us
  transfers between devices with their start and end apart: 105, of which 39 were waited for; matrix products, arithmetic and copies ran while one was open for 15% of the time, Pallas kernels for 0%

commit v1 on v0

v1 whole, which is shorter than its diff:
```python
import math

import jax
import jax.numpy as jnp
from jax import lax
from jax.experimental import pallas as pl
from jax.experimental.pallas import tpu as pltpu
from jax.sharding import PartitionSpec as P

HEAD = 128
BLOCK = 128
WINDOW = 9
CHUNK = 9
GROUP = 7
OWN = 5
PLACE_ROWS = 8
AXES = ("dp", "ctx", "kvh")
MASKED_LOGIT = -1e30


def dot_nt(a, b):
    return lax.dot_general(a, b, (((1,), (1,)), ((), ())), preferred_element_type=jnp.float32)


def dot_nn(a, b):
    return jnp.dot(a, b, preferred_element_type=jnp.float32)


def slots_of(place):
    lanes = lax.broadcasted_iota(jnp.int32, (BLOCK, BLOCK), 1)
    subs = lax.broadcasted_iota(jnp.int32, (BLOCK, BLOCK), 0)
    earlier = jnp.where(subs < lanes, 1.0, 0.0).astype(jnp.bfloat16)
    hits = [jnp.where(place == float(e), 1.0, 0.0) for e in range(16)]
    counts = dot_nn(jnp.concatenate(hits, axis=0).astype(jnp.bfloat16), earlier)
    slot = place * 16.0
    for e in range(16):
        slot = slot + hits[e] * counts[e * 16:(e + 1) * 16, :]
    return slot


def one_hot_slots(slot):
    slots = lax.broadcasted_iota(jnp.int32, (256, BLOCK), 0).astype(jnp.float32)
    return jnp.where(slot == slots, 1.0, 0.0).astype(jnp.bfloat16)


def attention_kernel(lengths, place, qd_a, qd_b, kv_own, kv_twin, sent, own_grad, twin_grad, box, k_all, v_all, q_all, g_all, w_all, s_all, logit, expo):
    heads = qd_a.shape[1] // (2 * HEAD)
    width = heads * HEAD
    half_rows = BLOCK // 2
    scaling = 1.0 / math.sqrt(HEAD)
    exponent = scaling * math.log2(math.e)
    group, ctx_pos, kvh_pos = (lax.axis_index(name) for name in AXES)
    off = kvh_pos * half_rows
    begin1 = lengths[0, group]
    begin2 = begin1 + lengths[1, group]
    begin3 = begin2 + lengths[2, group]
    lane = lax.broadcasted_iota(jnp.int32, (1, BLOCK), 1)
    position = ctx_pos * BLOCK + (lane ^ off)
    start = jnp.where(
        position >= begin3,
        begin3,
        jnp.where(position >= begin2, begin2, jnp.where(position >= begin1, begin1, 0)),
    )
    first = (ctx_pos - (WINDOW - 1)) * BLOCK
    row = lax.broadcasted_iota(jnp.int32, (BLOCK, BLOCK), 0)
    for t in range(WINDOW):
        block = jnp.maximum(ctx_pos - (WINDOW - 1) + t, 0)
        kv = kv_own if t % 2 == 0 else kv_twin
        for part in range(2):
            rows = slice(t * BLOCK + part * half_rows, t * BLOCK + (part + 1) * half_rows)
            k_all[rows, :] = kv[2 * (block // 2) + part, 0:half_rows, 0:HEAD]
            v_all[rows, :] = kv[2 * (block // 2) + part, 0:half_rows, HEAD:2 * HEAD]
    box[...] = slots_of(place[...])
    own = box[pl.ds(ctx_pos // 2, 1), :]
    own = jnp.where(off == 0, own, jnp.concatenate([own[:, half_rows:], own[:, :half_rows]], axis=1))
    slots = one_hot_slots(own)
    key_t = k_all[...].T
    value_t = v_all[...].T
    for h in range(heads):
        cols = slice(h * HEAD, (h + 1) * HEAD)
        gcols = slice(width + h * HEAD, width + (h + 1) * HEAD)
        q_all[cols, :] = jnp.concatenate([qd_a[:, cols], qd_b[:, cols]], axis=0)
        g_all[cols, :] = jnp.concatenate([qd_a[:, gcols], qd_b[:, gcols]], axis=0)

    def folded(x, op):
        x = x.reshape(x.shape[0] // 8, 8, x.shape[1])
        out = x[0]
        for i in range(1, x.shape[0]):
            out = op(out, x[i])
        return out

    span = CHUNK * BLOCK
    chunk_at = [slice(t * span, (t + 1) * span) for t in range(WINDOW // CHUNK)]
    wide = lax.broadcasted_iota(jnp.int32, (span, BLOCK), 0)
    for h in range(0, heads, GROUP):
        n = min(GROUP, heads - h)
        cols = slice(h * HEAD, (h + n) * HEAD)
        q, g = q_all[cols, :], g_all[cols, :]
        top = None
        for t, rows in enumerate(chunk_at):
            x = dot_nt(k_all[rows, :], q)
            base = first + t * span
            visible = wide >= start - base
            if t == len(chunk_at) - 1:
                visible = visible & (wide <= position - base)
            x = jnp.where(jnp.concatenate([visible] * n, axis=1), x, MASKED_LOGIT)
            logit[rows, :n * HEAD] = x
            x = folded(x, jnp.maximum)
            top = x if top is None else jnp.maximum(top, x)
        top = jnp.max(top, axis=0, keepdims=True)
        total = None
        for t, rows in enumerate(chunk_at):
            x = jnp.exp2((logit[rows, :n * HEAD] - top) * exponent)
            expo[rows, :n * HEAD] = x
            x = folded(x, jnp.add)
            total = x if total is None else total + x
        inverse = 1.0 / jnp.sum(total, axis=0, keepdims=True)
        for t, rows in enumerate(chunk_at):
            w_all[rows, cols] = (expo[rows, :n * HEAD] * inverse).astype(jnp.bfloat16)
        out_b = dot_nn(value_t, w_all[:, cols]).astype(jnp.bfloat16)
        stacked = jnp.concatenate([out_b[:, i * HEAD:(i + 1) * HEAD] for i in range(n)], axis=0)
        sent[:, cols] = dot_nt(slots, stacked).astype(jnp.bfloat16)
        g_t = g.astype(jnp.float32).T
        delta = jnp.sum(g_t * out_b.astype(jnp.float32), axis=0, keepdims=True)
        for t, rows in enumerate(chunk_at):
            dprob = dot_nt(v_all[rows, :], g)
            s_all[rows, cols] = ((expo[rows, :n * HEAD] * inverse) * (dprob - delta)).astype(jnp.bfloat16)
        dq_b = (dot_nn(key_t, s_all[:, cols]) * scaling).astype(jnp.bfloat16)
        stacked = jnp.concatenate([dq_b[:, i * HEAD:(i + 1) * HEAD] for i in range(n)], axis=0)
        sent[:, width + h * HEAD:width + (h + n) * HEAD] = dot_nt(slots, stacked).astype(jnp.bfloat16)
    q_rows = q_all[...]
    g_rows = g_all[...]
    grad_k = dot_nn(s_all[...], q_rows) * scaling
    grad_v = dot_nn(w_all[...], g_rows)
    for t in range(WINDOW):
        rows = slice(t * BLOCK, (t + 1) * BLOCK)
        step = WINDOW - 1 - t
        out = twin_grad if step % 2 else own_grad
        at = slice(step // 2 * BLOCK, (step // 2 + 1) * BLOCK)
        out[at, :HEAD] = grad_k[rows, :].astype(out.dtype)
        out[at, HEAD:] = grad_v[rows, :].astype(out.dtype)


def slots_kernel(box, rows_sent, own_grad, twin_grad, sent):
    ctx_pos = lax.axis_index(AXES[1])
    odd = ctx_pos % 2 == 1
    width = rows_sent.shape[1]
    sent[:, :width] = rows_sent[...]
    for i in range(OWN):
        total = own_grad[i * BLOCK:(i + 1) * BLOCK, :]
        zero = jnp.zeros(total.shape, jnp.float32)
        later = twin_grad[(i - 1) * BLOCK:i * BLOCK, :].astype(jnp.float32) if i > 0 else zero
        level = twin_grad[i * BLOCK:(i + 1) * BLOCK, :].astype(jnp.float32) if i < OWN - 1 else zero
        total = total + jnp.where(odd, later, level)
        block = jnp.maximum(ctx_pos - 2 * i, 0)
        hot = one_hot_slots(box[pl.ds(block // 2, 1), :])
        at = width + i * 2 * HEAD
        sent[:, at:at + 2 * HEAD] = dot_nn(hot, total.astype(jnp.bfloat16)).astype(jnp.bfloat16)


def landing_kernel(got, attended, grad_query, key_gradient, value_gradient):
    width = attended.shape[1]
    rows = got.shape[0]
    attended[...] = got[:, :width]
    grad_query[...] = got[:, width:2 * width]
    for b in range(16):
        total = jnp.zeros((16, 2 * HEAD), jnp.float32)
        for i in range(OWN):
            c = b + 2 * i
            at = 2 * width + i * 2 * HEAD
            if c < 16:
                total = total + got[c * 16:(c + 1) * 16, at:at + 2 * HEAD].astype(jnp.float32)
        key_gradient[b * 16:(b + 1) * 16, :] = total[:, :HEAD].astype(jnp.bfloat16)
        value_gradient[b * 16:(b + 1) * 16, :] = total[:, HEAD:].astype(jnp.bfloat16)


def pack_kernel(queries, grads, keys, values, place, kv, qd_a, qd_b):
    rows, width = queries.shape
    half = width // 2
    marks = jnp.broadcast_to(place[...].astype(jnp.float32).reshape(1, BLOCK), (PLACE_ROWS, BLOCK)).astype(jnp.bfloat16)
    marks = jnp.concatenate([marks, marks], axis=1)
    for k in range(kv.shape[0]):
        cols = slice(k * HEAD, (k + 1) * HEAD)
        kv[k] = jnp.concatenate([jnp.concatenate([keys[:, cols], values[:, cols]], axis=1), marks], axis=0)
    first = lax.axis_index("kvh") == 0
    for array, at in ((queries, 0), (grads, half)):
        low, high = array[:, :half], array[:, half:]
        qd_a[:, at:at + half] = jnp.where(first, low, high)
        qd_b[:, at:at + half] = jnp.where(first, high, low)


def copy_kernel(x, y):
    y[...] = x[...]


def shards(query_heads, key_heads, pool_values, output_grad, lengths, placement):
    dp_count, ctx_count, kvh_count = (lax.axis_size(name) for name in AXES)
    bf16, f32 = jnp.bfloat16, jnp.float32

    def place_of(d, c, k):
        return (d * ctx_count + c) * kvh_count + k

    def moved(value, target):
        pairs = [
            (place_of(d, c, k), place_of(*target(d, c, k)))
            for d in range(dp_count)
            for c in range(ctx_count)
            for k in range(kvh_count)
        ]
        return lax.ppermute(value, AXES, pairs)

    def to_group(d, c, k):
        return (d + c) % dp_count, c, k

    def to_group_swapped(d, c, k):
        return (d + c) % dp_count, c, k ^ 1

    rows = key_heads.shape[0]
    half_cols = query_heads.shape[1] // 2
    smem = pl.BlockSpec(memory_space=pltpu.SMEM)
    vmem = pl.BlockSpec(memory_space=pltpu.VMEM)
    params = pltpu.CompilerParams(vmem_limit_bytes=48 * 1024 * 1024)
    kv, qd_a, qd_b = pl.pallas_call(
        pack_kernel,
        out_shape=(
            jax.ShapeDtypeStruct((kvh_count, rows + PLACE_ROWS, 2 * HEAD), bf16),
            jax.ShapeDtypeStruct((rows, 2 * half_cols), bf16),
            jax.ShapeDtypeStruct((rows, 2 * half_cols), bf16),
        ),
        in_specs=[vmem] * 5,
        out_specs=(vmem,) * 3,
        name="pack",
    )(query_heads, output_grad, key_heads, pool_values, placement)
    kv = moved(kv, to_group)
    held = pl.pallas_call(
        copy_kernel,
        out_shape=jax.ShapeDtypeStruct((16, HEAD), bf16),
        in_specs=[pl.BlockSpec(memory_space=pltpu.VMEM)],
        out_specs=pl.BlockSpec(memory_space=pltpu.VMEM),
        cost_estimate=pl.CostEstimate(flops=13800000000, bytes_accessed=300000, transcendentals=0),
        name="hold",
    )(kv[0, :16, :HEAD])
    kv, held = lax.optimization_barrier((kv, held))
    qd_a = moved(qd_a, to_group)
    qd_b = moved(qd_b, to_group_swapped)
    half_count = ctx_count // 2
    copies = jnp.broadcast_to(kv[None], (half_count,) + kv.shape)
    copies = copies.reshape((ctx_count,) + kv.shape[1:])
    parities = [
        [c * kvh_count + k for c in range(parity, ctx_count, 2) for k in range(kvh_count)] for parity in range(2)
    ]
    to_twin = [(c, c ^ 1) for c in range(ctx_count)]

    def gathered(copies):
        kv = lax.all_to_all(
            copies, ("ctx", "kvh"), split_axis=0, concat_axis=0, axis_index_groups=parities, tiled=True
        )
        return kv, lax.ppermute(kv, "ctx", to_twin)

    kv, kv_twin = lax.cond(lax.axis_index(AXES[0]) >= 0, gathered, lambda copies: (copies, copies), copies)

    def marks_of(a):
        return a.reshape((half_count, kvh_count) + a.shape[1:])[:, 0, rows, :BLOCK].astype(f32)

    place = jnp.concatenate([marks_of(kv), marks_of(kv_twin)], axis=0)
    keys = WINDOW * BLOCK
    sent, own_grad, twin_grad, box = pl.pallas_call(
        attention_kernel,
        out_shape=(
            jax.ShapeDtypeStruct((256, 2 * half_cols), bf16),
            jax.ShapeDtypeStruct((OWN * BLOCK, 2 * HEAD), f32),
            jax.ShapeDtypeStruct(((WINDOW - OWN) * BLOCK, 2 * HEAD), bf16),
            jax.ShapeDtypeStruct((ctx_count, BLOCK), f32),
        ),
        in_specs=[smem] + [vmem] * 5,
        out_specs=(vmem,) * 4,
        scratch_shapes=[
            pltpu.VMEM((keys, HEAD), bf16),
            pltpu.VMEM((keys, HEAD), bf16),
            pltpu.VMEM((half_cols, HEAD), bf16),
            pltpu.VMEM((half_cols, HEAD), bf16),
            pltpu.VMEM((keys, half_cols), bf16),
            pltpu.VMEM((keys, half_cols), bf16),
            pltpu.VMEM((keys, GROUP * HEAD), f32),
            pltpu.VMEM((keys, GROUP * HEAD), f32),
        ],
        compiler_params=params,
        name="attention",
    )(lengths.T, place, qd_a, qd_b, kv, kv_twin)
    twin_grad = lax.ppermute(twin_grad, "ctx", to_twin)
    sent = pl.pallas_call(
        slots_kernel,
        out_shape=jax.ShapeDtypeStruct((256, 2 * half_cols + OWN * 2 * HEAD), bf16),
        in_specs=[vmem] * 4,
        out_specs=vmem,
        compiler_params=params,
        name="slots",
    )(box, sent, own_grad, twin_grad)
    boxes = sent.reshape(ctx_count, 16, sent.shape[1])
    got = lax.all_to_all(boxes, "ctx", split_axis=0, concat_axis=0, tiled=True)
    return pl.pallas_call(
        landing_kernel,
        out_shape=(
            jax.ShapeDtypeStruct((256, half_cols), bf16),
            jax.ShapeDtypeStruct((256, half_cols), bf16),
            jax.ShapeDtypeStruct((256, HEAD), bf16),
            jax.ShapeDtypeStruct((256, HEAD), bf16),
        ),
        in_specs=[vmem],
        out_specs=(vmem,) * 4,
        compiler_params=params,
        name="landing",
    )(got.reshape(256, -1))


def solution(mesh):
    in_specs = (
        P(AXES, None),
        P(AXES, None),
        P(AXES, None),
        P(AXES, None),
        P(),
        P(("dp", "ctx")),
    )
    out_specs = (P(("dp", "ctx"), "kvh"),) * 4
    return jax.shard_map(shards, mesh=mesh, in_specs=in_specs, out_specs=out_specs, check_vma=False)
```

time: 704 us -> 80.4 us (0.11)
  starting transfers between devices: 239 us -> 17 us
  blocking collectives: 195 us -> 49.3 us
  waiting for transfers between devices: 111 us -> 2.89 us
  matrix products: 65.8 us -> 0 us
  local copies, waits for them, and re-layouts: 36.7 us -> 0.82 us
  other arithmetic: 32.6 us -> 0.01 us
  between operations: 14.5 us -> 0.72 us
  Pallas kernels: 0 us -> 9.29 us
    ppermute x96 -> x5, starting transfers between devices: 202 us -> 17 us  [the longest x3 10.6 us: moved(): return lax.ppermute(value, AXES, pairs)]
    all_to_all x3 -> x2, blocking collectives: 151 us -> 49.3 us  [the longest x1 29.8 us: shards(): got = lax.all_to_all(boxes, 'ctx', split_axis=0, concat_axis=0, tiled=True)]
    dot_general x82 -> x0, matrix products: 65.8 us -> none  [the longest x17 22 us: logits_for(): jnp.einsum('qjgd,kjd->jgqk', query_split, key_split, preferred_element_ty...]
    all_to_all x7 -> x0, waiting for transfers between devices: 60 us -> none  [the longest x1 28 us: shards(): lax.all_to_all(spread(outgoing[3]), ('dp', 'ctx'), split_axis=0, concat_a...]
    ppermute x96 -> x5, waiting for transfers between devices: 51.3 us -> 2.89 us  [the longest x1 1.72 us: gathered(): return (kv, lax.ppermute(kv, 'ctx', to_twin))]
    all_gather x2 -> x0, blocking collectives: 44.4 us -> none  [the longest x1 24.5 us: shards(): lax.all_gather(for_sending(start_slots), 'ctx', axis=0, tiled=True)]
    all_to_all x7 -> x0, starting transfers between devices: 36.8 us -> none  [the longest x1 9.9 us: shards(): lax.all_to_all(spread(outgoing[3]), ('dp', 'ctx'), split_axis=0, concat_a...]
    gather x12 -> x0, local copies, waits for them, and re-layouts: 17.1 us -> none  [the longest x6 9.09 us: shards(): arrived = [jnp.take(member, chosen, axis=0) for member in landed]]
  transfers between devices with their start and end apart: 105 -> 5, of which waited for: 39 -> 2; matrix products, arithmetic and copies ran while one was open for 15% -> 1% of each run, Pallas kernels for 0% -> 0%
where the time goes in v1:
time: 80.4 us; the launch traced here: 80 us
  blocking collectives  49.3 us (61%)
  starting transfers between devices  17 us (21%)
  Pallas kernels  9.29 us (12%)
  waiting for transfers between devices  2.89 us (4%)
  local copies, waits for them, and re-layouts  0.82 us (1%)
    all_to_all x1, blocking collectives, shards(): got = lax.all_to_all(boxes, 'ctx', split_axis=0, concat_axis=0, tiled=True)  29.8 us
    all_to_all x1, blocking collectives, gathered(): lax.all_to_all(copies, ('ctx', 'kvh'), split_axis=0, concat_axis=0, axis_...  19.4 us
    ppermute x3, starting transfers between devices, moved(): return lax.ppermute(value, AXES, pairs)  10.6 us
    ppermute x1, starting transfers between devices, gathered(): return (kv, lax.ppermute(kv, 'ctx', to_twin))  5.89 us
    pallas_call x1, Pallas kernels, shards(): pl.pallas_call(attention_kernel, out_shape=(jax.ShapeDtypeStruct((256, 2...  5.89 us
    pallas_call x1, Pallas kernels, shards(): pl.pallas_call(pack_kernel, out_shape=(jax.ShapeDtypeStruct((kvh_count, r...  1.9 us
    ppermute x1, waiting for transfers between devices, gathered(): return (kv, lax.ppermute(kv, 'ctx', to_twin))  1.72 us
  transfers between devices with their start and end apart: 5, of which 2 were waited for; matrix products, arithmetic and copies ran while one was open for 1% of the time, Pallas kernels for 0%

profile of v1, /device:TPU:1, one launch (start us, length us, event | category | flops | bytes accessed | tf_op | source)
XLA Modules:
  0.0 80.0 jit_solution(6052761155133810984)
XLA Ops:
  0.6 1.9 %pack.1 = (bf16[2,72,256]{2,1,0:T(8,128)(2,1)}, bf16[64,1792]{1,0:T(8,128)(2,1)}, bf16[64,1792]{1,0:T(8,128)(2,1)}) custom-call(bf16[64,1792]{1,0:T(8,128)(2,1)} %queries.1, bf16[64,1792]{1,0:T(8,128)(2,1)} %grads.1, bf16[64,256]{1,0:T(8,128)(2,1)} %keys.1, bf16[64,256]{1,0:T(8,128)(2,1)} %values.1, s32[128]{0:T(128)} %place.1), custom_call_target="tpu_custom_call" | custom-call | tf_op jit(solution)/shard_map/pack/pallas_call | solution.py:223
  2.5 4.4 %collective-permute-start.1 = (bf16[2,72,256]{2,1,0:T(8,128)(2,1)}, bf16[2,72,256]{2,1,0:T(8,128)(2,1)S(1)}, u32[]{:S(2)}, u32[]{:S(2)}) collective-permute-start(bf16[2,72,256]{2,1,0:T(8,128)(2,1)} %get-tuple-element.15), channel_id=1, source_target_pairs={{0,0},{1,1},{2,34},{3,35},{4,68},{5,69},{6,102},{7,103},{8,136},{9... | collective-permute-start | bytes 221192 | tf_op jit(solution)/shard_map/ppermute | solution.py:210
  6.9 3.5 %collective-permute-start.2 = (bf16[64,1792]{1,0:T(8,128)(2,1)}, bf16[64,1792]{1,0:T(8,128)(2,1)S(1)}, u32[]{:S(2)}, u32[]{:S(2)}) collective-permute-start(bf16[64,1792]{1,0:T(8,128)(2,1)} %get-tuple-element.18), channel_id=1, source_target_pairs={{0,0},{1,1},{2,34},{3,35},{4,68},{5,69},{6,102},{7,103},{8,136},{9... | collective-permute-start | bytes 688136 | tf_op jit(solution)/shard_map/ppermute | solution.py:210
  10.5 2.7 %collective-permute-start.3 = (bf16[64,1792]{1,0:T(8,128)(2,1)}, bf16[64,1792]{1,0:T(8,128)(2,1)S(1)}, u32[]{:S(2)}, u32[]{:S(2)}) collective-permute-start(bf16[64,1792]{1,0:T(8,128)(2,1)} %get-tuple-element.19), channel_id=1, source_target_pairs={{0,1},{1,0},{2,35},{3,34},{4,69},{5,68},{6,103},{7,102},{8,137},{9... | collective-permute-start | bytes 688136 | tf_op jit(solution)/shard_map/ppermute | solution.py:210
  13.2 0.0 collective-permute-done.1
  13.2 0.0 copy-start
  13.2 27.1 %conditional.1 = (bf16[16,72,256]{2,1,0:T(8,128)(2,1)S(1)}, bf16[16,72,256]{2,1,0:T(8,128)(2,1)}) conditional(s32[]{:T(128)} %convert_element_type.11, bf16[16,72,256]{2,1,0:T(8,128)(2,1)S(1)} %bitcast.13, bf16[16,72,256]{2,1,0:T(8,128)(2,1)S(1)} %bitcast.14), branch_computations={%region_0.0_spmd, %region_1.0_spmd} | conditional | bytes 4718648 | solution.py:260
  13.2 19.4 %all_to_all.9 = bf16[16,72,256]{2,1,0:T(8,128)(2,1)S(1)} all-to-all(bf16[16,72,256]{2,1,0:T(8,128)(2,1)S(1)} %param.1), channel_id=1, replica_groups={{0,1,4,5,8,9,12,13,16,17,20,21,24,25,28,29},{2,3,6,7,10,11,14,15,18,19,..., dimensions={0} | all-to-all | bytes 1179648 | tf_op jit(solution)/shard_map/cond/branch_1_fun/all_to_all | solution.py:255
  32.7 5.9 %collective-permute-start = (bf16[16,72,256]{2,1,0:T(8,128)(2,1)S(1)}, bf16[16,72,256]{2,1,0:T(8,128)(2,1)}, u32[]{:S(2)}, u32[]{:S(2)}) collective-permute-start(bf16[16,72,256]{2,1,0:T(8,128)(2,1)S(1)} %all_to_all.9), channel_id=1, source_target_pairs={{0,2},{2,0},{4,6},{6,4},{8,10},{10,8},{12,14},{14,12},{16,18},{18,... | collective-permute-start | bytes 1769480 | tf_op jit(solution)/shard_map/cond/branch_1_fun/ppermute | solution.py:258
  38.6 1.7 %collective-permute-done = bf16[16,72,256]{2,1,0:T(8,128)(2,1)} collective-permute-done((bf16[16,72,256]{2,1,0:T(8,128)(2,1)S(1)}, bf16[16,72,256]{2,1,0:T(8,128)(2,1)}, u32[]{:S(2)}, u32[]{:S(2)}) %collective-permute-start) | collective-permute-done | bytes 589856 | tf_op jit(solution)/shard_map/cond/branch_1_fun/ppermute | solution.py:258
  40.3 0.7 slice.10
  41.1 0.0 collective-permute-done.2.qd_a
  41.1 0.0 collective-permute-done.3.qd_b
  41.1 0.0 copy-done
  41.1 5.9 %attention.1 = (bf16[256,1792]{1,0:T(8,128)(2,1)S(1)}, f32[640,256]{1,0:T(8,128)S(1)}, bf16[512,256]{1,0:T(8,128)(2,1)S(1)}, f32[16,128]{1,0:T(8,128)S(1)}) custom-call(s32[4,8]{1,0:T(4,128)S(1)} %bitcast.12, f32[16,128]{1,0:T(8,128)S(1)} %maximum_convert_fusion.place, bf16[64,1792]{1,0:T(8,128)(2,1)S(1)} %collective-permute-done.2.qd_a, ...), custom_call_target="tpu_custom_call" | custom-call | tf_op jit(solution)/shard_map/attention/pallas_call | solution.py:267
  47.0 0.5 collective-permute-start.4
  47.5 1.2 %collective-permute-done.4.twin_grad = bf16[512,256]{1,0:T(8,128)(2,1)S(1)} collective-permute-done((bf16[512,256]{1,0:T(8,128)(2,1)S(1)}, bf16[512,256]{1,0:T(8,128)(2,1)S(1)}, u32[]{:S(2)}, u32[]{:S(2)}) %collective-permute-start.4) | collective-permute-done | bytes 262176 | tf_op jit(solution)/shard_map/ppermute | solution.py:290
  48.6 0.5 slots.1
  49.1 29.8 %all_to_all.10 = bf16[16,16,3072]{2,1,0:T(8,128)(2,1)S(1)} all-to-all(bf16[16,16,3072]{2,1,0:T(8,128)(2,1)S(1)} %bitcast.11), channel_id=1, replica_groups=mesh['dp'=8,'ctx'=16,'kvh'=2] {'ctx'}, dimensions={0} | all-to-all | bytes 3145728 | tf_op jit(solution)/shard_map/all_to_all | solution.py:300
  78.9 1.0 %landing.1 = (bf16[256,896]{1,0:T(8,128)(2,1)}, bf16[256,896]{1,0:T(8,128)(2,1)}, bf16[256,128]{1,0:T(8,128)(2,1)}, bf16[256,128]{1,0:T(8,128)(2,1)}) custom-call(bf16[256,3072]{1,0:T(8,128)(2,1)S(1)} %bitcast.10), custom_call_target="tpu_custom_call" | custom-call | tf_op jit(solution)/shard_map/landing/pallas_call | solution.py:301
  (5 shorter events, 0.1 us)
Async XLA Ops:
  2.5 10.7 %collective-permute-start.1 = (bf16[2,72,256]{2,1,0:T(8,128)(2,1)}, bf16[2,72,256]{2,1,0:T(8,128)(2,1)S(1)}, u32[]{:S(2)}, u32[]{:S(2)}) collective-permute-start(bf16[2,72,256]{2,1,0:T(8,128)(2,1)} %get-tuple-element.15), channel_id=1, source_target_pairs={{0,0},{1,1},{2,34},{3,35},{4,68},{5,69},{6,102},{7,103},{8,136},{9... | collective-permute-start | bytes 221192 | tf_op jit(solution)/shard_map/ppermute | solution.py:210
  6.9 34.2 %collective-permute-start.2 = (bf16[64,1792]{1,0:T(8,128)(2,1)}, bf16[64,1792]{1,0:T(8,128)(2,1)S(1)}, u32[]{:S(2)}, u32[]{:S(2)}) collective-permute-start(bf16[64,1792]{1,0:T(8,128)(2,1)} %get-tuple-element.18), channel_id=1, source_target_pairs={{0,0},{1,1},{2,34},{3,35},{4,68},{5,69},{6,102},{7,103},{8,136},{9... | collective-permute-start | bytes 688136 | tf_op jit(solution)/shard_map/ppermute | solution.py:210
  10.5 30.7 %collective-permute-start.3 = (bf16[64,1792]{1,0:T(8,128)(2,1)}, bf16[64,1792]{1,0:T(8,128)(2,1)S(1)}, u32[]{:S(2)}, u32[]{:S(2)}) collective-permute-start(bf16[64,1792]{1,0:T(8,128)(2,1)} %get-tuple-element.19), channel_id=1, source_target_pairs={{0,1},{1,0},{2,35},{3,34},{4,69},{5,68},{6,103},{7,102},{8,137},{9... | collective-permute-start | bytes 688136 | tf_op jit(solution)/shard_map/ppermute | solution.py:210
  13.2 27.9 %copy-start = (s32[8,4]{0,1:T(4,128)S(1)}, s32[8,4]{0,1:T(4,128)}, u32[]{:S(2)}) copy-start(s32[8,4]{0,1:T(4,128)} %param.12) | copy-start | bytes 388
  32.7 7.7 %collective-permute-start = (bf16[16,72,256]{2,1,0:T(8,128)(2,1)S(1)}, bf16[16,72,256]{2,1,0:T(8,128)(2,1)}, u32[]{:S(2)}, u32[]{:S(2)}) collective-permute-start(bf16[16,72,256]{2,1,0:T(8,128)(2,1)S(1)} %all_to_all.9), channel_id=1, source_target_pairs={{0,2},{2,0},{4,6},{6,4},{8,10},{10,8},{12,14},{14,12},{16,18},{18,... | collective-permute-start | bytes 1769480 | tf_op jit(solution)/shard_map/cond/branch_1_fun/ppermute | solution.py:258
  47.0 1.6 %collective-permute-start.4 = (bf16[512,256]{1,0:T(8,128)(2,1)S(1)}, bf16[512,256]{1,0:T(8,128)(2,1)S(1)}, u32[]{:S(2)}, u32[]{:S(2)}) collective-permute-start(bf16[512,256]{1,0:T(8,128)(2,1)S(1)} %get-tuple-element.23), channel_id=1, source_target_pairs={{0,2},{2,0},{4,6},{6,4},{8,10},{10,8},{12,14},{14,12},{16,18},{18,... | collective-permute-start | bytes 786440 | tf_op jit(solution)/shard_map/ppermute | solution.py:290

commit v2 on v1

--- a/solution.py
+++ b/solution.py
@@ -10,7 +10,7 @@
 HEAD = 128
 BLOCK = 128
 WINDOW = 9
-CHUNK = 9
+CHUNK = 3
 GROUP = 7
 OWN = 5
 PLACE_ROWS = 8
@@ -43,7 +43,9 @@
     return jnp.where(slot == slots, 1.0, 0.0).astype(jnp.bfloat16)
 
 
-def attention_kernel(lengths, place, qd_a, qd_b, kv_own, kv_twin, sent, own_grad, twin_grad, box, k_all, v_all, q_all, g_all, w_all, s_all, logit, expo):
+def attention_kernel(
+    lengths, qd_a, qd_b, kv_own, kv_twin, rows_t, own_grad, twin_grad, box, k_all, s_all, v_all, q_all, g_all, w_all, logit, expo
+):
     heads = qd_a.shape[1] // (2 * HEAD)
     width = heads * HEAD
     half_rows = BLOCK // 2
@@ -70,11 +72,10 @@
             rows = slice(t * BLOCK + part * half_rows, t * BLOCK + (part + 1) * half_rows)
             k_all[rows, :] = kv[2 * (block // 2) + part, 0:half_rows, 0:HEAD]
             v_all[rows, :] = kv[2 * (block // 2) + part, 0:half_rows, HEAD:2 * HEAD]
-    box[...] = slots_of(place[...])
-    own = box[pl.ds(ctx_pos // 2, 1), :]
-    own = jnp.where(off == 0, own, jnp.concatenate([own[:, half_rows:], own[:, :half_rows]], axis=1))
-    slots = one_hot_slots(own)
-    key_t = k_all[...].T
+    marks = [
+        kv[2 * j, :, 0:HEAD].astype(jnp.float32)[half_rows:half_rows + 1, :] for kv in (kv_own, kv_twin) for j in range(8)
+    ]
+    box[...] = slots_of(jnp.concatenate(marks, axis=0))
     value_t = v_all[...].T
     for h in range(heads):
         cols = slice(h * HEAD, (h + 1) * HEAD)
@@ -104,30 +105,26 @@
             if t == len(chunk_at) - 1:
                 visible = visible & (wide <= position - base)
             x = jnp.where(jnp.concatenate([visible] * n, axis=1), x, MASKED_LOGIT)
-            logit[rows, :n * HEAD] = x
+            logit[rows, cols] = x
             x = folded(x, jnp.maximum)
             top = x if top is None else jnp.maximum(top, x)
         top = jnp.max(top, axis=0, keepdims=True)
         total = None
         for t, rows in enumerate(chunk_at):
-            x = jnp.exp2((logit[rows, :n * HEAD] - top) * exponent)
-            expo[rows, :n * HEAD] = x
+            x = jnp.exp2((logit[rows, cols] - top) * exponent)
+            expo[rows, cols] = x
             x = folded(x, jnp.add)
             total = x if total is None else total + x
         inverse = 1.0 / jnp.sum(total, axis=0, keepdims=True)
         for t, rows in enumerate(chunk_at):
-            w_all[rows, cols] = (expo[rows, :n * HEAD] * inverse).astype(jnp.bfloat16)
+            w_all[rows, cols] = (expo[rows, cols] * inverse).astype(jnp.bfloat16)
         out_b = dot_nn(value_t, w_all[:, cols]).astype(jnp.bfloat16)
-        stacked = jnp.concatenate([out_b[:, i * HEAD:(i + 1) * HEAD] for i in range(n)], axis=0)
-        sent[:, cols] = dot_nt(slots, stacked).astype(jnp.bfloat16)
+        rows_t[:, cols] = out_b
         g_t = g.astype(jnp.float32).T
         delta = jnp.sum(g_t * out_b.astype(jnp.float32), axis=0, keepdims=True)
         for t, rows in enumerate(chunk_at):
             dprob = dot_nt(v_all[rows, :], g)
-            s_all[rows, cols] = ((expo[rows, :n * HEAD] * inverse) * (dprob - delta)).astype(jnp.bfloat16)
-        dq_b = (dot_nn(key_t, s_all[:, cols]) * scaling).astype(jnp.bfloat16)
-        stacked = jnp.concatenate([dq_b[:, i * HEAD:(i + 1) * HEAD] for i in range(n)], axis=0)
-        sent[:, width + h * HEAD:width + (h + n) * HEAD] = dot_nt(slots, stacked).astype(jnp.bfloat16)
+            s_all[rows, cols] = ((expo[rows, cols] * inverse) * (dprob - delta)).astype(jnp.bfloat16)
     q_rows = q_all[...]
     g_rows = g_all[...]
     grad_k = dot_nn(s_all[...], q_rows) * scaling
@@ -141,11 +138,24 @@
         out[at, HEAD:] = grad_v[rows, :].astype(out.dtype)
 
 
-def slots_kernel(box, rows_sent, own_grad, twin_grad, sent):
+def row_slots_kernel(box, rows_t, k_all, s_all, sent):
+    ctx_pos, kvh_pos = lax.axis_index(AXES[1]), lax.axis_index(AXES[2])
+    half_rows = BLOCK // 2
+    own = box[pl.ds(ctx_pos // 2, 1), :]
+    own = jnp.where(kvh_pos == 0, own, jnp.concatenate([own[:, half_rows:], own[:, :half_rows]], axis=1))
+    slots = one_hot_slots(own)
+    grads_t = (dot_nn(k_all[...].T, s_all[...]) * (1.0 / math.sqrt(HEAD))).astype(jnp.bfloat16)
+    count = rows_t.shape[1] // HEAD
+    stacked = jnp.concatenate(
+        [a[:, i * HEAD:(i + 1) * HEAD] for a in (rows_t[...], grads_t) for i in range(count)], axis=0
+    )
+    sent[:, :2 * rows_t.shape[1]] = dot_nt(slots, stacked).astype(jnp.bfloat16)
+
+
+def grad_slots_kernel(box, begun, own_grad, twin_grad, sent):
     ctx_pos = lax.axis_index(AXES[1])
     odd = ctx_pos % 2 == 1
-    width = rows_sent.shape[1]
-    sent[:, :width] = rows_sent[...]
+    width = sent.shape[1] - OWN * 2 * HEAD
     for i in range(OWN):
         total = own_grad[i * BLOCK:(i + 1) * BLOCK, :]
         zero = jnp.zeros(total.shape, jnp.float32)
@@ -189,8 +199,9 @@
         qd_b[:, at:at + half] = jnp.where(first, high, low)
 
 
-def copy_kernel(x, y):
-    y[...] = x[...]
+def copies_kernel(kv, copies):
+    for i in range(copies.shape[0]):
+        copies[i] = kv[i % kv.shape[0]]
 
 
 def shards(query_heads, key_heads, pool_values, output_grad, lengths, placement):
@@ -212,8 +223,11 @@
     def to_group(d, c, k):
         return (d + c) % dp_count, c, k
 
-    def to_group_swapped(d, c, k):
-        return (d + c) % dp_count, c, k ^ 1
+    def aside(d, c, k):
+        return d, c ^ 4, k ^ 1
+
+    def to_group_from_aside(d, c, k):
+        return to_group(d, c ^ 4, k)
 
     rows = key_heads.shape[0]
     half_cols = query_heads.shape[1] // 2
@@ -223,29 +237,26 @@
     kv, qd_a, qd_b = pl.pallas_call(
         pack_kernel,
         out_shape=(
-            jax.ShapeDtypeStruct((kvh_count, rows + PLACE_ROWS, 2 * HEAD), bf16),
-            jax.ShapeDtypeStruct((rows, 2 * half_cols), bf16),
-            jax.ShapeDtypeStruct((rows, 2 * half_cols), bf16),
+            pltpu.VMEM((kvh_count, rows + PLACE_ROWS, 2 * HEAD), bf16),
+            pltpu.VMEM((rows, 2 * half_cols), bf16),
+            pltpu.VMEM((rows, 2 * half_cols), bf16),
         ),
         in_specs=[vmem] * 5,
         out_specs=(vmem,) * 3,
         name="pack",
     )(query_heads, output_grad, key_heads, pool_values, placement)
     kv = moved(kv, to_group)
-    held = pl.pallas_call(
-        copy_kernel,
-        out_shape=jax.ShapeDtypeStruct((16, HEAD), bf16),
-        in_specs=[pl.BlockSpec(memory_space=pltpu.VMEM)],
-        out_specs=pl.BlockSpec(memory_space=pltpu.VMEM),
+    qd_a = moved(qd_a, to_group)
+    qd_b = moved(moved(qd_b, aside), to_group_from_aside)
+    copies = pl.pallas_call(
+        copies_kernel,
+        out_shape=jax.ShapeDtypeStruct((ctx_count,) + kv.shape[1:], bf16),
+        in_specs=[vmem],
+        out_specs=vmem,
         cost_estimate=pl.CostEstimate(flops=13800000000, bytes_accessed=300000, transcendentals=0),
-        name="hold",
-    )(kv[0, :16, :HEAD])
-    kv, held = lax.optimization_barrier((kv, held))
-    qd_a = moved(qd_a, to_group)
-    qd_b = moved(qd_b, to_group_swapped)
-    half_count = ctx_count // 2
-    copies = jnp.broadcast_to(kv[None], (half_count,) + kv.shape)
-    copies = copies.reshape((ctx_count,) + kv.shape[1:])
+        compiler_params=params,
+        name="copies",
+    )(kv)
     parities = [
         [c * kvh_count + k for c in range(parity, ctx_count, 2) for k in range(kvh_count)] for parity in range(2)
     ]
@@ -259,42 +270,48 @@
 
     kv, kv_twin = lax.cond(lax.axis_index(AXES[0]) >= 0, gathered, lambda copies: (copies, copies), copies)
 
-    def marks_of(a):
-        return a.reshape((half_count, kvh_count) + a.shape[1:])[:, 0, rows, :BLOCK].astype(f32)
-
-    place = jnp.concatenate([marks_of(kv), marks_of(kv_twin)], axis=0)
     keys = WINDOW * BLOCK
-    sent, own_grad, twin_grad, box = pl.pallas_call(
+    rows_t, own_grad, twin_grad, box, k_all, s_all = pl.pallas_call(
         attention_kernel,
         out_shape=(
-            jax.ShapeDtypeStruct((256, 2 * half_cols), bf16),
-            jax.ShapeDtypeStruct((OWN * BLOCK, 2 * HEAD), f32),
-            jax.ShapeDtypeStruct(((WINDOW - OWN) * BLOCK, 2 * HEAD), bf16),
-            jax.ShapeDtypeStruct((ctx_count, BLOCK), f32),
+            pltpu.VMEM((HEAD, half_cols), bf16),
+            pltpu.VMEM((OWN * BLOCK, 2 * HEAD), f32),
+            pltpu.VMEM(((WINDOW - OWN) * BLOCK, 2 * HEAD), bf16),
+            pltpu.VMEM((ctx_count, BLOCK), f32),
+            pltpu.VMEM((keys, HEAD), bf16),
+            pltpu.VMEM((keys, half_cols), bf16),
         ),
-        in_specs=[smem] + [vmem] * 5,
-        out_specs=(vmem,) * 4,
+        in_specs=[smem] + [vmem] * 4,
+        out_specs=(vmem,) * 6,
         scratch_shapes=[
-            pltpu.VMEM((keys, HEAD), bf16),
             pltpu.VMEM((keys, HEAD), bf16),
             pltpu.VMEM((half_cols, HEAD), bf16),
             pltpu.VMEM((half_cols, HEAD), bf16),
             pltpu.VMEM((keys, half_cols), bf16),
-            pltpu.VMEM((keys, half_cols), bf16),
-            pltpu.VMEM((keys, GROUP * HEAD), f32),
-            pltpu.VMEM((keys, GROUP * HEAD), f32),
+            pltpu.VMEM((keys, 7 * HEAD), f32),
+            pltpu.VMEM((keys, 7 * HEAD), f32),
         ],
         compiler_params=params,
         name="attention",
-    )(lengths.T, place, qd_a, qd_b, kv, kv_twin)
+    )(lengths.T, qd_a, qd_b, kv, kv_twin)
     twin_grad = lax.ppermute(twin_grad, "ctx", to_twin)
+    sent_shape = jax.ShapeDtypeStruct((256, 2 * half_cols + OWN * 2 * HEAD), bf16)
     sent = pl.pallas_call(
-        slots_kernel,
-        out_shape=jax.ShapeDtypeStruct((256, 2 * half_cols + OWN * 2 * HEAD), bf16),
+        row_slots_kernel,
+        out_shape=sent_shape,
         in_specs=[vmem] * 4,
         out_specs=vmem,
         compiler_params=params,
-        name="slots",
+        name="row_slots",
+    )(box, rows_t, k_all, s_all)
+    sent = pl.pallas_call(
+        grad_slots_kernel,
+        out_shape=sent_shape,
+        in_specs=[vmem, pl.BlockSpec(memory_space=pl.ANY), vmem, vmem],
+        out_specs=vmem,
+        input_output_aliases={1: 0},
+        compiler_params=params,
+        name="grad_slots",
     )(box, sent, own_grad, twin_grad)
     boxes = sent.reshape(ctx_count, 16, sent.shape[1])
     got = lax.all_to_all(boxes, "ctx", split_axis=0, concat_axis=0, tiled=True)

time: 80.4 us -> 76.6 us (0.953)
  blocking collectives: 49.3 us -> 42.4 us
  starting transfers between devices: 17 us -> 22.6 us
  waiting for transfers between devices: 2.89 us -> 2.08 us
    ppermute x3 -> x4, starting transfers between devices: 10.6 us -> 17.9 us  [moved(): return lax.ppermute(value, AXES, pairs)]
    all_to_all x1, blocking collectives: 19.4 us -> 15.1 us  [gathered(): lax.all_to_all(copies, ('ctx', 'kvh'), split_axis=0, concat_axis=0, axis_...]
    all_to_all x1, blocking collectives: 29.8 us -> 27.3 us  [shards(): got = lax.all_to_all(boxes, 'ctx', split_axis=0, concat_axis=0, tiled=True)]
    ppermute x1, starting transfers between devices: 5.89 us -> 4.15 us  [gathered(): return (kv, lax.ppermute(kv, 'ctx', to_twin))]
    ppermute x1, waiting for transfers between devices: 1.16 us -> 0.35 us  [shards(): twin_grad = lax.ppermute(twin_grad, 'ctx', to_twin)]
    pallas_call x3 -> x5, Pallas kernels: 8.24 us -> 7.52 us  [the longest x1 5.21 us: shards(): pl.pallas_call(attention_kernel, out_shape=(pltpu.VMEM((HEAD, half_cols),...]
  transfers between devices with their start and end apart: 5 -> 6, of which waited for: 2 -> 2; matrix products, arithmetic and copies ran while one was open for 1% -> 0% of each run, Pallas kernels for 0% -> 1%
where the time goes in v2:
time: 76.6 us; the launch traced here: 76.4 us
  blocking collectives  42.4 us (55%)
  starting transfers between devices  22.6 us (30%)
  Pallas kernels  8.56 us (11%)
  waiting for transfers between devices  2.08 us (3%)
    all_to_all x1, blocking collectives, shards(): got = lax.all_to_all(boxes, 'ctx', split_axis=0, concat_axis=0, tiled=True)  27.3 us
    ppermute x4, starting transfers between devices, moved(): return lax.ppermute(value, AXES, pairs)  17.9 us
    all_to_all x1, blocking collectives, gathered(): lax.all_to_all(copies, ('ctx', 'kvh'), split_axis=0, concat_axis=0, axis_...  15.1 us
    pallas_call x1, Pallas kernels, shards(): pl.pallas_call(attention_kernel, out_shape=(pltpu.VMEM((HEAD, half_cols),...  5.21 us
    ppermute x1, starting transfers between devices, gathered(): return (kv, lax.ppermute(kv, 'ctx', to_twin))  4.15 us
    ppermute x1, waiting for transfers between devices, gathered(): return (kv, lax.ppermute(kv, 'ctx', to_twin))  1.72 us
  transfers between devices with their start and end apart: 6, of which 2 were waited for; matrix products, arithmetic and copies ran while one was open for 0% of the time, Pallas kernels for 1%

profile of v2, /device:TPU:1, one launch (start us, length us, event | category | flops | bytes accessed | tf_op | source)
XLA Modules:
  0.0 76.4 jit_solution(955102460316777164)
XLA Ops:
  0.6 1.1 %pack.1 = (bf16[2,72,256]{2,1,0:T(8,128)(2,1)S(1)}, bf16[64,1792]{1,0:T(8,128)(2,1)S(1)}, bf16[64,1792]{1,0:T(8,128)(2,1)S(1)}) custom-call(bf16[64,1792]{1,0:T(8,128)(2,1)} %queries.1, bf16[64,1792]{1,0:T(8,128)(2,1)} %grads.1, bf16[64,256]{1,0:T(8,128)(2,1)} %keys.1, bf16[64,256]{1,0:T(8,128)(2,1)} %values.1, s32[128]{0:T(128)} %place.1), custom_call_target="tpu_custom_call" | custom-call | tf_op jit(solution)/shard_map/pack/pallas_call | solution.py:237
  1.8 3.1 %collective-permute-start.2 = (bf16[64,1792]{1,0:T(8,128)(2,1)S(1)}, bf16[64,1792]{1,0:T(8,128)(2,1)S(1)}, u32[]{:S(2)}, u32[]{:S(2)}) collective-permute-start(bf16[64,1792]{1,0:T(8,128)(2,1)S(1)} %get-tuple-element.18), channel_id=1, source_target_pairs={{0,9},{1,8},{2,11},{3,10},{4,13},{5,12},{6,15},{7,14},{8,1},{9,0},... | collective-permute-start | bytes 688136 | tf_op jit(solution)/shard_map/ppermute | solution.py:221
  4.9 3.5 %collective-permute-start.4 = (bf16[2,72,256]{2,1,0:T(8,128)(2,1)S(1)}, bf16[2,72,256]{2,1,0:T(8,128)(2,1)S(1)}, u32[]{:S(2)}, u32[]{:S(2)}) collective-permute-start(bf16[2,72,256]{2,1,0:T(8,128)(2,1)S(1)} %get-tuple-element.19), channel_id=1, source_target_pairs={{0,0},{1,1},{2,34},{3,35},{4,68},{5,69},{6,102},{7,103},{8,136},{9... | collective-permute-start | bytes 221192 | tf_op jit(solution)/shard_map/ppermute | solution.py:221
  8.4 3.5 %collective-permute-start.1 = (bf16[64,1792]{1,0:T(8,128)(2,1)S(1)}, bf16[64,1792]{1,0:T(8,128)(2,1)S(1)}, u32[]{:S(2)}, u32[]{:S(2)}) collective-permute-start(bf16[64,1792]{1,0:T(8,128)(2,1)S(1)} %get-tuple-element.17), channel_id=1, source_target_pairs={{0,0},{1,1},{2,34},{3,35},{4,68},{5,69},{6,102},{7,103},{8,136},{9... | collective-permute-start | bytes 688136 | tf_op jit(solution)/shard_map/ppermute | solution.py:221
  12.0 0.0 collective-permute-done.2
  12.0 7.7 %collective-permute-start.3 = (bf16[64,1792]{1,0:T(8,128)(2,1)S(1)}, bf16[64,1792]{1,0:T(8,128)(2,1)S(1)}, u32[]{:S(2)}, u32[]{:S(2)}) collective-permute-start(bf16[64,1792]{1,0:T(8,128)(2,1)S(1)} %collective-permute-done.2), channel_id=1, source_target_pairs={{0,136},{1,137},{2,170},{3,171},{4,204},{5,205},{6,238},{7,239},{8... | collective-permute-start | bytes 688136 | tf_op jit(solution)/shard_map/ppermute | solution.py:221
  19.7 0.0 collective-permute-done.4.kv
  19.8 0.0 copy-start
  19.8 21.0 %conditional.1 = (bf16[16,72,256]{2,1,0:T(8,128)(2,1)S(1)}, bf16[16,72,256]{2,1,0:T(8,128)(2,1)}) conditional(s32[]{:T(128)} %convert_element_type.3, bf16[16,72,256]{2,1,0:T(8,128)(2,1)S(1)} %copies.1, bf16[16,72,256]{2,1,0:T(8,128)(2,1)S(1)} %copies.1), branch_computations={%region_0.0_spmd, %region_1.0_spmd} | conditional | bytes 4718648 | solution.py:271
  19.8 15.1 %all_to_all.9 = bf16[16,72,256]{2,1,0:T(8,128)(2,1)S(1)} all-to-all(bf16[16,72,256]{2,1,0:T(8,128)(2,1)S(1)} %param.1), channel_id=1, replica_groups={{0,1,4,5,8,9,12,13,16,17,20,21,24,25,28,29},{2,3,6,7,10,11,14,15,18,19,..., dimensions={0} | all-to-all | bytes 1179648 | tf_op jit(solution)/shard_map/cond/branch_1_fun/all_to_all | solution.py:266
  34.9 4.2 %collective-permute-start = (bf16[16,72,256]{2,1,0:T(8,128)(2,1)S(1)}, bf16[16,72,256]{2,1,0:T(8,128)(2,1)}, u32[]{:S(2)}, u32[]{:S(2)}) collective-permute-start(bf16[16,72,256]{2,1,0:T(8,128)(2,1)S(1)} %all_to_all.9), channel_id=1, source_target_pairs={{0,2},{2,0},{4,6},{6,4},{8,10},{10,8},{12,14},{14,12},{16,18},{18,... | collective-permute-start | bytes 1769480 | tf_op jit(solution)/shard_map/cond/branch_1_fun/ppermute | solution.py:269
  39.1 1.7 %collective-permute-done = bf16[16,72,256]{2,1,0:T(8,128)(2,1)} collective-permute-done((bf16[16,72,256]{2,1,0:T(8,128)(2,1)S(1)}, bf16[16,72,256]{2,1,0:T(8,128)(2,1)}, u32[]{:S(2)}, u32[]{:S(2)}) %collective-permute-start) | collective-permute-done | bytes 589856 | tf_op jit(solution)/shard_map/cond/branch_1_fun/ppermute | solution.py:269
  40.8 0.0 collective-permute-done.1.qd_a
  40.8 0.0 collective-permute-done.3.qd_b
  40.8 0.0 copy-done
  40.8 5.2 %attention.1 = (bf16[128,896]{1,0:T(8,128)(2,1)S(1)}, f32[640,256]{1,0:T(8,128)S(1)}, bf16[512,256]{1,0:T(8,128)(2,1)S(1)}, f32[16,128]{1,0:T(8,128)S(1)}, bf16[...) custom-call(s32[4,8]{1,0:T(4,128)S(1)} %bitcast.5, bf16[64,1792]{1,0:T(8,128)(2,1)S(1)} %collective-permute-done.1.qd_a, ...), custom_call_target="tpu_custom_call" | custom-call | tf_op jit(solution)/shard_map/attention/pallas_call | solution.py:274
  46.0 0.5 collective-permute-start.5
  46.5 0.8 %row_slots.1.begun = bf16[256,3072]{1,0:T(8,128)(2,1)S(1)} custom-call(f32[16,128]{1,0:T(8,128)S(1)} %get-tuple-element.22.box, bf16[128,896]{1,0:T(8,128)(2,1)S(1)} %get-tuple-element.23.rows_t, bf16[1152,128]{1,0:T(8,128)(2,1)S(1)} %get-tuple-element.24.k_all, bf16[1152,896]{1,0:T(8,128)(2,1)S(1)} %get-tuple-element.25.s_all), custom_call_target="tpu_custom_call" | custom-call | tf_op jit(solution)/shard_map/row_slots/pallas_call | solution.py:299
  47.3 0.3 collective-permute-done.5.twin_grad
  47.7 0.3 grad_slots.1
  48.0 27.3 %all_to_all.10 = bf16[16,16,3072]{2,1,0:T(8,128)(2,1)S(1)} all-to-all(bf16[16,16,3072]{2,1,0:T(8,128)(2,1)S(1)} %bitcast.3), channel_id=1, replica_groups=mesh['dp'=8,'ctx'=16,'kvh'=2] {'ctx'}, dimensions={0} | all-to-all | bytes 3145728 | tf_op jit(solution)/shard_map/all_to_all | solution.py:317
  75.3 1.0 %landing.1 = (bf16[256,896]{1,0:T(8,128)(2,1)}, bf16[256,896]{1,0:T(8,128)(2,1)}, bf16[256,128]{1,0:T(8,128)(2,1)}, bf16[256,128]{1,0:T(8,128)(2,1)}) custom-call(bf16[256,3072]{1,0:T(8,128)(2,1)S(1)} %bitcast.4), custom_call_target="tpu_custom_call" | custom-call | tf_op jit(solution)/shard_map/landing/pallas_call | solution.py:318
  (2 shorter events, 0.1 us)
Async XLA Ops:
  1.8 10.2 %collective-permute-start.2 = (bf16[64,1792]{1,0:T(8,128)(2,1)S(1)}, bf16[64,1792]{1,0:T(8,128)(2,1)S(1)}, u32[]{:S(2)}, u32[]{:S(2)}) collective-permute-start(bf16[64,1792]{1,0:T(8,128)(2,1)S(1)} %get-tuple-element.18), channel_id=1, source_target_pairs={{0,9},{1,8},{2,11},{3,10},{4,13},{5,12},{6,15},{7,14},{8,1},{9,0},... | collective-permute-start | bytes 688136 | tf_op jit(solution)/shard_map/ppermute | solution.py:221
  4.9 14.8 %collective-permute-start.4 = (bf16[2,72,256]{2,1,0:T(8,128)(2,1)S(1)}, bf16[2,72,256]{2,1,0:T(8,128)(2,1)S(1)}, u32[]{:S(2)}, u32[]{:S(2)}) collective-permute-start(bf16[2,72,256]{2,1,0:T(8,128)(2,1)S(1)} %get-tuple-element.19), channel_id=1, source_target_pairs={{0,0},{1,1},{2,34},{3,35},{4,68},{5,69},{6,102},{7,103},{8,136},{9... | collective-permute-start | bytes 221192 | tf_op jit(solution)/shard_map/ppermute | solution.py:221
  8.4 32.4 %collective-permute-start.1 = (bf16[64,1792]{1,0:T(8,128)(2,1)S(1)}, bf16[64,1792]{1,0:T(8,128)(2,1)S(1)}, u32[]{:S(2)}, u32[]{:S(2)}) collective-permute-start(bf16[64,1792]{1,0:T(8,128)(2,1)S(1)} %get-tuple-element.17), channel_id=1, source_target_pairs={{0,0},{1,1},{2,34},{3,35},{4,68},{5,69},{6,102},{7,103},{8,136},{9... | collective-permute-start | bytes 688136 | tf_op jit(solution)/shard_map/ppermute | solution.py:221
  12.0 28.8 %collective-permute-start.3 = (bf16[64,1792]{1,0:T(8,128)(2,1)S(1)}, bf16[64,1792]{1,0:T(8,128)(2,1)S(1)}, u32[]{:S(2)}, u32[]{:S(2)}) collective-permute-start(bf16[64,1792]{1,0:T(8,128)(2,1)S(1)} %collective-permute-done.2), channel_id=1, source_target_pairs={{0,136},{1,137},{2,170},{3,171},{4,204},{5,205},{6,238},{7,239},{8... | collective-permute-start | bytes 688136 | tf_op jit(solution)/shard_map/ppermute | solution.py:221
  19.8 21.0 %copy-start = (s32[8,4]{0,1:T(4,128)S(1)}, s32[8,4]{0,1:T(4,128)}, u32[]{:S(2)}) copy-start(s32[8,4]{0,1:T(4,128)} %param.12) | copy-start | bytes 388
  34.9 5.9 %collective-permute-start = (bf16[16,72,256]{2,1,0:T(8,128)(2,1)S(1)}, bf16[16,72,256]{2,1,0:T(8,128)(2,1)}, u32[]{:S(2)}, u32[]{:S(2)}) collective-permute-start(bf16[16,72,256]{2,1,0:T(8,128)(2,1)S(1)} %all_to_all.9), channel_id=1, source_target_pairs={{0,2},{2,0},{4,6},{6,4},{8,10},{10,8},{12,14},{14,12},{16,18},{18,... | collective-permute-start | bytes 1769480 | tf_op jit(solution)/shard_map/cond/branch_1_fun/ppermute | solution.py:269
  46.0 1.6 %collective-permute-start.5 = (bf16[512,256]{1,0:T(8,128)(2,1)S(1)}, bf16[512,256]{1,0:T(8,128)(2,1)S(1)}, u32[]{:S(2)}, u32[]{:S(2)}) collective-permute-start(bf16[512,256]{1,0:T(8,128)(2,1)S(1)} %get-tuple-element.27), channel_id=1, source_target_pairs={{0,2},{2,0},{4,6},{6,4},{8,10},{10,8},{12,14},{14,12},{16,18},{18,... | collective-permute-start | bytes 786440 | tf_op jit(solution)/shard_map/ppermute | solution.py:297

commit v3 on v2

--- a/solution.py
+++ b/solution.py
@@ -33,8 +33,9 @@
     hits = [jnp.where(place == float(e), 1.0, 0.0) for e in range(16)]
     counts = dot_nn(jnp.concatenate(hits, axis=0).astype(jnp.bfloat16), earlier)
     slot = place * 16.0
+    blocks = place.shape[0]
     for e in range(16):
-        slot = slot + hits[e] * counts[e * 16:(e + 1) * 16, :]
+        slot = slot + hits[e] * counts[e * blocks:(e + 1) * blocks, :]
     return slot
 
 
@@ -73,7 +74,7 @@
             k_all[rows, :] = kv[2 * (block // 2) + part, 0:half_rows, 0:HEAD]
             v_all[rows, :] = kv[2 * (block // 2) + part, 0:half_rows, HEAD:2 * HEAD]
     marks = [
-        kv[2 * j, :, 0:HEAD].astype(jnp.float32)[half_rows:half_rows + 1, :] for kv in (kv_own, kv_twin) for j in range(8)
+        kv[2 * j, :, 0:HEAD].astype(jnp.float32)[half_rows:half_rows + 1, :] for kv in (kv_own,) for j in range(8)
     ]
     box[...] = slots_of(jnp.concatenate(marks, axis=0))
     value_t = v_all[...].T
@@ -277,7 +278,7 @@
             pltpu.VMEM((HEAD, half_cols), bf16),
             pltpu.VMEM((OWN * BLOCK, 2 * HEAD), f32),
             pltpu.VMEM(((WINDOW - OWN) * BLOCK, 2 * HEAD), bf16),
-            pltpu.VMEM((ctx_count, BLOCK), f32),
+            pltpu.VMEM((ctx_count // 2, BLOCK), f32),
             pltpu.VMEM((keys, HEAD), bf16),
             pltpu.VMEM((keys, half_cols), bf16),
         ),

time: 76.6 us -> 76.6 us (level)
  no operation moved by 1% of the time
where the time goes in v3:
time: 76.6 us; the launch traced here: 76.3 us
  blocking collectives  42.4 us (55%)
  starting transfers between devices  22.6 us (30%)
  Pallas kernels  8.53 us (11%)
  waiting for transfers between devices  2.07 us (3%)
    all_to_all x1, blocking collectives, shards(): got = lax.all_to_all(boxes, 'ctx', split_axis=0, concat_axis=0, tiled=True)  27.3 us
    ppermute x4, starting transfers between devices, moved(): return lax.ppermute(value, AXES, pairs)  17.9 us
    all_to_all x1, blocking collectives, gathered(): lax.all_to_all(copies, ('ctx', 'kvh'), split_axis=0, concat_axis=0, axis_...  15.1 us
    pallas_call x1, Pallas kernels, shards(): pl.pallas_call(attention_kernel, out_shape=(pltpu.VMEM((HEAD, half_cols),...  5.17 us
    ppermute x1, starting transfers between devices, gathered(): return (kv, lax.ppermute(kv, 'ctx', to_twin))  4.15 us
    ppermute x1, waiting for transfers between devices, gathered(): return (kv, lax.ppermute(kv, 'ctx', to_twin))  1.72 us
  transfers between devices with their start and end apart: 6, of which 2 were waited for; matrix products, arithmetic and copies ran while one was open for 0% of the time, Pallas kernels for 1%

profile of v3, /device:TPU:1, one launch (start us, length us, event | category | flops | bytes accessed | tf_op | source)
XLA Modules:
  0.0 76.3 jit_solution(9903207244029842112)
XLA Ops:
  0.6 1.1 %pack.1 = (bf16[2,72,256]{2,1,0:T(8,128)(2,1)S(1)}, bf16[64,1792]{1,0:T(8,128)(2,1)S(1)}, bf16[64,1792]{1,0:T(8,128)(2,1)S(1)}) custom-call(bf16[64,1792]{1,0:T(8,128)(2,1)} %queries.1, bf16[64,1792]{1,0:T(8,128)(2,1)} %grads.1, bf16[64,256]{1,0:T(8,128)(2,1)} %keys.1, bf16[64,256]{1,0:T(8,128)(2,1)} %values.1, s32[128]{0:T(128)} %place.1), custom_call_target="tpu_custom_call" | custom-call | tf_op jit(solution)/shard_map/pack/pallas_call | solution.py:238
  1.8 3.1 %collective-permute-start.2 = (bf16[64,1792]{1,0:T(8,128)(2,1)S(1)}, bf16[64,1792]{1,0:T(8,128)(2,1)S(1)}, u32[]{:S(2)}, u32[]{:S(2)}) collective-permute-start(bf16[64,1792]{1,0:T(8,128)(2,1)S(1)} %get-tuple-element.18), channel_id=1, source_target_pairs={{0,9},{1,8},{2,11},{3,10},{4,13},{5,12},{6,15},{7,14},{8,1},{9,0},... | collective-permute-start | bytes 688136 | tf_op jit(solution)/shard_map/ppermute | solution.py:222
  4.9 3.5 %collective-permute-start.4 = (bf16[2,72,256]{2,1,0:T(8,128)(2,1)S(1)}, bf16[2,72,256]{2,1,0:T(8,128)(2,1)S(1)}, u32[]{:S(2)}, u32[]{:S(2)}) collective-permute-start(bf16[2,72,256]{2,1,0:T(8,128)(2,1)S(1)} %get-tuple-element.19), channel_id=1, source_target_pairs={{0,0},{1,1},{2,34},{3,35},{4,68},{5,69},{6,102},{7,103},{8,136},{9... | collective-permute-start | bytes 221192 | tf_op jit(solution)/shard_map/ppermute | solution.py:222
  8.4 3.5 %collective-permute-start.1 = (bf16[64,1792]{1,0:T(8,128)(2,1)S(1)}, bf16[64,1792]{1,0:T(8,128)(2,1)S(1)}, u32[]{:S(2)}, u32[]{:S(2)}) collective-permute-start(bf16[64,1792]{1,0:T(8,128)(2,1)S(1)} %get-tuple-element.17), channel_id=1, source_target_pairs={{0,0},{1,1},{2,34},{3,35},{4,68},{5,69},{6,102},{7,103},{8,136},{9... | collective-permute-start | bytes 688136 | tf_op jit(solution)/shard_map/ppermute | solution.py:222
  12.0 0.0 collective-permute-done.2
  12.0 7.7 %collective-permute-start.3 = (bf16[64,1792]{1,0:T(8,128)(2,1)S(1)}, bf16[64,1792]{1,0:T(8,128)(2,1)S(1)}, u32[]{:S(2)}, u32[]{:S(2)}) collective-permute-start(bf16[64,1792]{1,0:T(8,128)(2,1)S(1)} %collective-permute-done.2), channel_id=1, source_target_pairs={{0,136},{1,137},{2,170},{3,171},{4,204},{5,205},{6,238},{7,239},{8... | collective-permute-start | bytes 688136 | tf_op jit(solution)/shard_map/ppermute | solution.py:222
  19.7 0.0 collective-permute-done.4.kv
  19.8 0.0 copy-start
  19.8 21.0 %conditional.1 = (bf16[16,72,256]{2,1,0:T(8,128)(2,1)S(1)}, bf16[16,72,256]{2,1,0:T(8,128)(2,1)}) conditional(s32[]{:T(128)} %convert_element_type.3, bf16[16,72,256]{2,1,0:T(8,128)(2,1)S(1)} %copies.1, bf16[16,72,256]{2,1,0:T(8,128)(2,1)S(1)} %copies.1), branch_computations={%region_0.0_spmd, %region_1.0_spmd} | conditional | bytes 4718648 | solution.py:272
  19.8 15.1 %all_to_all.9 = bf16[16,72,256]{2,1,0:T(8,128)(2,1)S(1)} all-to-all(bf16[16,72,256]{2,1,0:T(8,128)(2,1)S(1)} %param.1), channel_id=1, replica_groups={{0,1,4,5,8,9,12,13,16,17,20,21,24,25,28,29},{2,3,6,7,10,11,14,15,18,19,..., dimensions={0} | all-to-all | bytes 1179648 | tf_op jit(solution)/shard_map/cond/branch_1_fun/all_to_all | solution.py:267
  34.9 4.2 %collective-permute-start = (bf16[16,72,256]{2,1,0:T(8,128)(2,1)S(1)}, bf16[16,72,256]{2,1,0:T(8,128)(2,1)}, u32[]{:S(2)}, u32[]{:S(2)}) collective-permute-start(bf16[16,72,256]{2,1,0:T(8,128)(2,1)S(1)} %all_to_all.9), channel_id=1, source_target_pairs={{0,2},{2,0},{4,6},{6,4},{8,10},{10,8},{12,14},{14,12},{16,18},{18,... | collective-permute-start | bytes 1769480 | tf_op jit(solution)/shard_map/cond/branch_1_fun/ppermute | solution.py:270
  39.1 1.7 %collective-permute-done = bf16[16,72,256]{2,1,0:T(8,128)(2,1)} collective-permute-done((bf16[16,72,256]{2,1,0:T(8,128)(2,1)S(1)}, bf16[16,72,256]{2,1,0:T(8,128)(2,1)}, u32[]{:S(2)}, u32[]{:S(2)}) %collective-permute-start) | collective-permute-done | bytes 589856 | tf_op jit(solution)/shard_map/cond/branch_1_fun/ppermute | solution.py:270
  40.8 0.0 collective-permute-done.1.qd_a
  40.8 0.0 collective-permute-done.3.qd_b
  40.8 0.0 copy-done
  40.8 5.2 %attention.1 = (bf16[128,896]{1,0:T(8,128)(2,1)S(1)}, f32[640,256]{1,0:T(8,128)S(1)}, bf16[512,256]{1,0:T(8,128)(2,1)S(1)}, f32[8,128]{1,0:T(8,128)S(1)}, bf16[1...) custom-call(s32[4,8]{1,0:T(4,128)S(1)} %bitcast.5, bf16[64,1792]{1,0:T(8,128)(2,1)S(1)} %collective-permute-done.1.qd_a, ...), custom_call_target="tpu_custom_call" | custom-call | tf_op jit(solution)/shard_map/attention/pallas_call | solution.py:275
  46.0 0.5 collective-permute-start.5
  46.4 0.8 %row_slots.1.begun = bf16[256,3072]{1,0:T(8,128)(2,1)S(1)} custom-call(f32[8,128]{1,0:T(8,128)S(1)} %get-tuple-element.22.box, bf16[128,896]{1,0:T(8,128)(2,1)S(1)} %get-tuple-element.23.rows_t, bf16[1152,128]{1,0:T(8,128)(2,1)S(1)} %get-tuple-element.24.k_all, bf16[1152,896]{1,0:T(8,128)(2,1)S(1)} %get-tuple-element.25.s_all), custom_call_target="tpu_custom_call" | custom-call | tf_op jit(solution)/shard_map/row_slots/pallas_call | solution.py:300
  47.3 0.3 collective-permute-done.5.twin_grad
  47.6 0.3 grad_slots.1
  48.0 27.3 %all_to_all.10 = bf16[16,16,3072]{2,1,0:T(8,128)(2,1)S(1)} all-to-all(bf16[16,16,3072]{2,1,0:T(8,128)(2,1)S(1)} %bitcast.3), channel_id=1, replica_groups=mesh['dp'=8,'ctx'=16,'kvh'=2] {'ctx'}, dimensions={0} | all-to-all | bytes 3145728 | tf_op jit(solution)/shard_map/all_to_all | solution.py:318
  75.3 1.0 %landing.1 = (bf16[256,896]{1,0:T(8,128)(2,1)}, bf16[256,896]{1,0:T(8,128)(2,1)}, bf16[256,128]{1,0:T(8,128)(2,1)}, bf16[256,128]{1,0:T(8,128)(2,1)}) custom-call(bf16[256,3072]{1,0:T(8,128)(2,1)S(1)} %bitcast.4), custom_call_target="tpu_custom_call" | custom-call | tf_op jit(solution)/shard_map/landing/pallas_call | solution.py:319
  (2 shorter events, 0.1 us)
Async XLA Ops:
  1.8 10.2 %collective-permute-start.2 = (bf16[64,1792]{1,0:T(8,128)(2,1)S(1)}, bf16[64,1792]{1,0:T(8,128)(2,1)S(1)}, u32[]{:S(2)}, u32[]{:S(2)}) collective-permute-start(bf16[64,1792]{1,0:T(8,128)(2,1)S(1)} %get-tuple-element.18), channel_id=1, source_target_pairs={{0,9},{1,8},{2,11},{3,10},{4,13},{5,12},{6,15},{7,14},{8,1},{9,0},... | collective-permute-start | bytes 688136 | tf_op jit(solution)/shard_map/ppermute | solution.py:222
  4.9 14.8 %collective-permute-start.4 = (bf16[2,72,256]{2,1,0:T(8,128)(2,1)S(1)}, bf16[2,72,256]{2,1,0:T(8,128)(2,1)S(1)}, u32[]{:S(2)}, u32[]{:S(2)}) collective-permute-start(bf16[2,72,256]{2,1,0:T(8,128)(2,1)S(1)} %get-tuple-element.19), channel_id=1, source_target_pairs={{0,0},{1,1},{2,34},{3,35},{4,68},{5,69},{6,102},{7,103},{8,136},{9... | collective-permute-start | bytes 221192 | tf_op jit(solution)/shard_map/ppermute | solution.py:222
  8.4 32.4 %collective-permute-start.1 = (bf16[64,1792]{1,0:T(8,128)(2,1)S(1)}, bf16[64,1792]{1,0:T(8,128)(2,1)S(1)}, u32[]{:S(2)}, u32[]{:S(2)}) collective-permute-start(bf16[64,1792]{1,0:T(8,128)(2,1)S(1)} %get-tuple-element.17), channel_id=1, source_target_pairs={{0,0},{1,1},{2,34},{3,35},{4,68},{5,69},{6,102},{7,103},{8,136},{9... | collective-permute-start | bytes 688136 | tf_op jit(solution)/shard_map/ppermute | solution.py:222
  12.0 28.8 %collective-permute-start.3 = (bf16[64,1792]{1,0:T(8,128)(2,1)S(1)}, bf16[64,1792]{1,0:T(8,128)(2,1)S(1)}, u32[]{:S(2)}, u32[]{:S(2)}) collective-permute-start(bf16[64,1792]{1,0:T(8,128)(2,1)S(1)} %collective-permute-done.2), channel_id=1, source_target_pairs={{0,136},{1,137},{2,170},{3,171},{4,204},{5,205},{6,238},{7,239},{8... | collective-permute-start | bytes 688136 | tf_op jit(solution)/shard_map/ppermute | solution.py:222
  19.8 21.0 %copy-start = (s32[8,4]{0,1:T(4,128)S(1)}, s32[8,4]{0,1:T(4,128)}, u32[]{:S(2)}) copy-start(s32[8,4]{0,1:T(4,128)} %param.12) | copy-start | bytes 388
  34.9 5.9 %collective-permute-start = (bf16[16,72,256]{2,1,0:T(8,128)(2,1)S(1)}, bf16[16,72,256]{2,1,0:T(8,128)(2,1)}, u32[]{:S(2)}, u32[]{:S(2)}) collective-permute-start(bf16[16,72,256]{2,1,0:T(8,128)(2,1)S(1)} %all_to_all.9), channel_id=1, source_target_pairs={{0,2},{2,0},{4,6},{6,4},{8,10},{10,8},{12,14},{14,12},{16,18},{18,... | collective-permute-start | bytes 1769480 | tf_op jit(solution)/shard_map/cond/branch_1_fun/ppermute | solution.py:270
  46.0 1.6 %collective-permute-start.5 = (bf16[512,256]{1,0:T(8,128)(2,1)S(1)}, bf16[512,256]{1,0:T(8,128)(2,1)S(1)}, u32[]{:S(2)}, u32[]{:S(2)}) collective-permute-start(bf16[512,256]{1,0:T(8,128)(2,1)S(1)} %get-tuple-element.27), channel_id=1, source_target_pairs={{0,2},{2,0},{4,6},{6,4},{8,10},{10,8},{12,14},{14,12},{16,18},{18,... | collective-permute-start | bytes 786440 | tf_op jit(solution)/shard_map/ppermute | solution.py:298
